TPU v7x, 512 devices: a whole 4x8x8 slice. The times are simulated.
512 devices in a mesh: head: 8 (over y), inner: 4 (over z_lo, core), outer: 16 (over z_hi, x).
Axes of the slice: x: 4, y: 8, z: 8 (z_hi: 4, z_lo: 2; z = z_hi * 2 + z_lo), core: 2. Of those that a mesh axis runs over, the one named last changes fastest.
Arguments:
- q_rows: bfloat16 [8192, 4096], P(('inner', 'outer', 'head')), may hold values from -8 to 8
- k_rows: bfloat16 [8192, 1024], P(('inner', 'outer', 'head')), may hold values from -8 to 8
- v_rows: bfloat16 [8192, 1024], P(('inner', 'outer', 'head')), may hold values from -6 to 6
- dout: bfloat16 [8192, 4096], P(('inner', 'outer'), 'head'), may hold values from -6 to 6
- positions: int32 [8192], replicated, may hold values from 0 to 8191, as said below
Outputs:
- attn_out: bfloat16 [8192, 4096], P(('inner', 'outer'), 'head')
- grad_q: bfloat16 [8192, 4096], P(('inner', 'outer'), 'head')
- grad_k: bfloat16 [8192, 1024], P(('inner', 'outer'), 'head')
- grad_v: bfloat16 [8192, 1024], P(('inner', 'outer'), 'head')
Inputs may be any that keep to these rules, and one draw needn't show every extreme that they name: A permutation of the positions. The rows of block b (rows b*128 to (b+1)*128 - 1) hold, in rising order, the positions p*128/2 to (p+1)*128/2-1 in their first half and (127-p)*128/2 onward in their second half, for a p below 64 that differs from block to block.
All inputs are finite; a program needn't handle non-finite values.
Results may differ from a plain program's by a relative error of at most 0.012.
Values may be sent and summed in bfloat16 or wider, within the bound.
A program may use at most 64 MiB of HBM per device.

v0:
```python
import jax
import jax.numpy as jnp
from jax import lax
from jax.sharding import PartitionSpec as P

QH = 32
KVH = 8
DH = 128


NEG_FILL = -1e30


def passed_along(x, axis, by):
    length = lax.axis_size(axis)
    return lax.ppermute(x, axis, [(i, (i + by) % length) for i in range(length)])


def forward_tile(carried, query_rows, query_pos, key_rows, value_rows, key_pos, score_scale):
    running_max, running_sum, weighted = carried
    scores = (
        jnp.einsum("qgrd,kgd->grqk", query_rows, key_rows, preferred_element_type=jnp.float32)
        * score_scale
    )
    visible = key_pos[None, :] <= query_pos[:, None]
    masked = jnp.where(visible, scores, NEG_FILL)
    new_max = jnp.maximum(running_max, jnp.max(masked, axis=-1))
    factor = jnp.exp(running_max - new_max)
    weights = jnp.where(visible, jnp.exp(masked - new_max[..., None]), 0.0)
    running_sum = running_sum * factor + jnp.sum(weights, axis=-1)
    weighted = weighted * factor[..., None] + jnp.einsum(
        "grqk,kgd->grqd", weights, value_rows.astype(jnp.float32), precision=lax.Precision.HIGHEST
    )
    return (new_max, running_sum, weighted)


def backward_tile(
    query_rows,
    grad_acc,
    upstream,
    log_sums,
    inner_prod,
    key_rows,
    value_rows,
    query_pos,
    key_pos,
    score_scale,
):
    scores = (
        jnp.einsum("qgrd,kgd->grqk", query_rows, key_rows, preferred_element_type=jnp.float32)
        * score_scale
    )
    visible = key_pos[None, :] <= query_pos[:, None]
    clipped = jnp.where(visible, scores, log_sums[..., None])
    prob_rounded = jnp.where(visible, jnp.exp(clipped - log_sums[..., None]), 0.0).astype(
        jnp.bfloat16
    )
    prob_rounded = lax.optimization_barrier(prob_rounded)
    dprobs = jnp.einsum("qgrd,kgd->grqk", upstream, value_rows, preferred_element_type=jnp.float32)
    dscores = (
        prob_rounded.astype(jnp.float32) * (dprobs - inner_prod[..., None]) * score_scale
    ).astype(jnp.bfloat16)
    grad_value = jnp.einsum(
        "grqk,qgrd->kgd", prob_rounded, upstream, preferred_element_type=jnp.float32
    )
    grad_key = jnp.einsum("grqk,qgrd->kgd", dscores, query_rows, preferred_element_type=jnp.float32)
    grad_acc = grad_acc + jnp.einsum(
        "grqk,kgd->qgrd", dscores, key_rows, preferred_element_type=jnp.float32
    )
    return (grad_acc, grad_key, grad_value)


def shards(q_rows, k_rows, v_rows, dout, positions):
    queries, keys_own, values_own = (
        lax.all_to_all(q_rows, "head", split_axis=1, concat_axis=0, tiled=True),
        lax.all_to_all(k_rows, "head", split_axis=1, concat_axis=0, tiled=True),
        lax.all_to_all(v_rows, "head", split_axis=1, concat_axis=0, tiled=True),
    )
    rows_here = queries.shape[0]
    half_rows = rows_here // 2
    groups = keys_own.shape[1] // DH
    head_ratio = QH // KVH
    kv_width = groups * DH
    score_scale = DH ** (-0.5)
    q_heads = queries.reshape(rows_here, groups, head_ratio, DH)
    d_heads = dout.reshape(rows_here, groups, head_ratio, DH)
    inner_count = lax.axis_size("inner")
    outer_count = lax.axis_size("outer")
    block_count = inner_count * outer_count
    inner_here = lax.axis_index("inner")
    outer_here = lax.axis_index("outer")
    own_block = inner_here * outer_count + outer_here
    query_pos = lax.dynamic_slice_in_dim(positions, own_block * rows_here, rows_here)
    held_block = jnp.concatenate([keys_own, values_own], axis=1)

    def unpack(kv_block):
        key_rows = kv_block[:, :kv_width].reshape(rows_here, groups, DH)
        value_rows = kv_block[:, kv_width:].reshape(rows_here, groups, DH)
        return (key_rows, value_rows)

    def visit(kv_block, block_index, states):
        key_rows, value_rows = unpack(kv_block)
        key_pos = lax.dynamic_slice_in_dim(positions, block_index * rows_here, rows_here)
        first_half = forward_tile(
            states[0],
            q_heads[:half_rows],
            query_pos[:half_rows],
            key_rows[:half_rows],
            value_rows[:half_rows],
            key_pos[:half_rows],
            score_scale,
        )
        second_half = forward_tile(
            states[1],
            q_heads[half_rows:],
            query_pos[half_rows:],
            key_rows,
            value_rows,
            key_pos,
            score_scale,
        )
        return (first_half, second_half)

    def backward_block(kv_block, block_index, grad_sums, grad_rows, saved_stats):
        key_rows, value_rows = unpack(kv_block)
        key_pos = lax.dynamic_slice_in_dim(positions, block_index * rows_here, rows_here)
        log_first, log_second, prod_first, prod_second = saved_stats
        grad_first, gk_first, gv_first = backward_tile(
            q_heads[:half_rows],
            grad_rows[0],
            d_heads[:half_rows],
            log_first,
            prod_first,
            key_rows[:half_rows],
            value_rows[:half_rows],
            query_pos[:half_rows],
            key_pos[:half_rows],
            score_scale,
        )
        grad_second, gk_second, gv_second = backward_tile(
            q_heads[half_rows:],
            grad_rows[1],
            d_heads[half_rows:],
            log_second,
            prod_second,
            key_rows,
            value_rows,
            query_pos[half_rows:],
            key_pos,
            score_scale,
        )
        grad_key = jnp.concatenate(
            [gk_second[:half_rows] + gk_first, gk_second[half_rows:]], axis=0
        )
        grad_value = jnp.concatenate(
            [gv_second[:half_rows] + gv_first, gv_second[half_rows:]], axis=0
        )
        grad_sums = grad_sums + jnp.concatenate(
            [grad_key.reshape(rows_here, kv_width), grad_value.reshape(rows_here, kv_width)], axis=1
        )
        return (grad_sums, (grad_first, grad_second))

    empty_max = jnp.full((groups, head_ratio, half_rows), NEG_FILL, jnp.float32)
    empty_sum = jnp.zeros((groups, head_ratio, half_rows), jnp.float32)
    empty_weighted = jnp.zeros((groups, head_ratio, half_rows, DH), jnp.float32)
    start_states = ((empty_max, empty_sum, empty_weighted), (empty_max, empty_sum, empty_weighted))
    zero_sums = jnp.zeros((rows_here, 2 * kv_width), jnp.float32)
    zero_grads = jnp.zeros((half_rows, groups, head_ratio, DH), jnp.float32)

    def forward_turn(turn_index, loop_state):
        kv_block, states = loop_state
        states = visit(kv_block, (own_block - turn_index) % block_count, states)
        kv_block = passed_along(kv_block, ("inner", "outer"), 1)
        return (kv_block, states)

    kv_block, states = lax.fori_loop(0, block_count - 1, forward_turn, (held_block, start_states))
    states = visit(kv_block, (own_block - (block_count - 1)) % block_count, states)
    outputs = []
    log_parts = []
    for running_max, running_sum, weighted in states:
        log_parts.append(running_max + jnp.log(running_sum))
        outputs.append(jnp.transpose(weighted / running_sum[..., None], (2, 0, 1, 3)))
    attn_heads = jnp.concatenate(outputs, axis=0).astype(jnp.bfloat16)
    attn_heads = lax.optimization_barrier(attn_heads)
    inner_prod = jnp.sum(d_heads.astype(jnp.float32) * attn_heads.astype(jnp.float32), axis=-1)
    inner_prod = jnp.transpose(inner_prod, (1, 2, 0))
    finish_saved_stats = (
        log_parts[0],
        log_parts[1],
        inner_prod[:, :, :half_rows],
        inner_prod[:, :, half_rows:],
    )
    attn_out = attn_heads.reshape(rows_here, groups * head_ratio * DH)
    saved_stats = finish_saved_stats

    def backward_turn(turn_index, loop_state):
        kv_block, grad_sums, grad_rows = loop_state
        distance = block_count - 1 - turn_index
        block_index = (own_block - distance) % block_count
        grad_sums, grad_rows = backward_block(
            kv_block, block_index, grad_sums, grad_rows, saved_stats
        )
        kv_block = passed_along(kv_block, ("inner", "outer"), -1)
        grad_sums = passed_along(grad_sums, ("inner", "outer"), -1)
        return (kv_block, grad_sums, grad_rows)

    kv_block, grad_sums, grad_rows = lax.fori_loop(
        0, block_count - 1, backward_turn, (kv_block, zero_sums, (zero_grads, zero_grads))
    )
    grad_sums, grad_rows = backward_block(kv_block, own_block, grad_sums, grad_rows, saved_stats)
    grad_q = (
        jnp.concatenate([grad_rows[0], grad_rows[1]], axis=0)
        .reshape(rows_here, groups * head_ratio * DH)
        .astype(jnp.bfloat16)
    )
    grad_k = grad_sums[:, :kv_width].astype(jnp.bfloat16)
    grad_v = grad_sums[:, kv_width:].astype(jnp.bfloat16)
    return (attn_out, grad_q, grad_k, grad_v)


def solution(mesh):
    return jax.shard_map(
        shards,
        mesh=mesh,
        in_specs=(
            P(("inner", "outer", "head"), None),
            P(("inner", "outer", "head"), None),
            P(("inner", "outer", "head"), None),
            P(("inner", "outer"), "head"),
            P(),
        ),
        out_specs=(
            P(("inner", "outer"), "head"),
            P(("inner", "outer"), "head"),
            P(("inner", "outer"), "head"),
            P(("inner", "outer"), "head"),
        ),
        check_vma=False,
    )
```

profile of v0, /device:TPU:1, one launch (start us, length us, event | category | flops | bytes accessed | tf_op | source)
XLA Modules:
  0.0 1831.0 jit_solution(18260482049210065779)
XLA Ops:
  30.3 7.7 all-to-all-done.2
  38.1 662.2 %while.50 = (s32[]{:T(128)}, bf16[128,256]{1,0:T(8,128)(2,1)S(1)}, f32[1,4,64]{2,1,0:T(4,128)S(1)}, f32[1,4,64]{2,1,0:T(4,128)S(1)}, f32[1,4,64,128]{3,2,1,0:T(8...) while((s32[]{:T(128)}, bf16[128,256]{1,0:T(8,128)(2,1)S(1)}, ...), condition=%wide.region_5.6_spmd.clone, body=%wide.region_0.5_spmd.clone.sunk | while | flops 88685584 | bytes 1900166 | solution.py:176
  43.7 13.5 collective-permute-done
  702.1 1123.8 %while.51 = (s32[]{:T(128)}, bf16[128,256]{1,0:T(8,128)(2,1)S(1)}, f32[128,256]{1,0:T(8,128)S(1)}, f32[64,1,4,128]{3,0,2,1:T(8,128)S(1)}, f32[64,1,4,128]{3,0,2,...) while((s32[]{:T(128)}, bf16[128,256]{1,0:T(8,128)(2,1)S(1)}, ...), condition=%wide.region_12.13_spmd.clone, body=%wide.region_11.12_spmd.clone.sunk | while | flops 63664144 | bytes 4218619 | solution.py:207
  729.9 8.0 collective-permute-start.1
  748.3 10.4 collective-permute-start.1
  773.4 8.6 collective-permute-start.1
  810.3 8.6 collective-permute-start.1
  828.8 10.1 collective-permute-start.1
  848.4 8.4 collective-permute-start.1
  866.4 8.2 collective-permute-start.1
  884.2 7.9 collective-permute-start.1
  901.7 8.3 collective-permute-start.1
  919.5 7.8 collective-permute-start.1
  936.9 8.1 collective-permute-start.1
  954.6 8.2 collective-permute-start.1
  972.3 8.2 collective-permute-start.1
  990.7 8.6 collective-permute-start.1
  1043.4 8.6 collective-permute-start.1
  1079.4 8.6 collective-permute-start.1
  1097.7 8.6 collective-permute-start.1
  1150.3 8.6 collective-permute-start.1
  1186.3 8.6 collective-permute-start.1
  1204.5 7.9 collective-permute-start.1
  1238.8 8.7 collective-permute-start.1
  1257.1 8.6 collective-permute-start.1
  1275.3 8.3 collective-permute-start.1
  1293.2 8.0 collective-permute-start.1
  1310.8 8.6 collective-permute-start.1
  1345.8 8.5 collective-permute-start.1
  1363.8 8.5 collective-permute-start.1
  1381.9 8.5 collective-permute-start.1
  1399.9 7.7 collective-permute-start.1
  1417.3 8.6 collective-permute-start.1
  1452.5 8.6 collective-permute-start.1
  1470.6 8.4 collective-permute-start.1
  1505.9 8.5 collective-permute-start.1
  1524.1 8.6 collective-permute-start.1
  1558.8 8.5 collective-permute-start.1
  1576.9 7.8 collective-permute-start.1
  1594.3 8.6 collective-permute-start.1
  1612.9 8.6 collective-permute-start.1
  1664.8 8.2 collective-permute-start.1
  1682.5 8.5 collective-permute-start.1
  1701.6 8.6 collective-permute-start.1
  1719.8 8.4 collective-permute-start.1
  1772.2 8.6 collective-permute-start.1
  1807.7 8.6 collective-permute-start.1
  (2801 shorter events, 1420.1 us)
Async XLA Ops:
  2.0 14.6 all-to-all-start
  38.2 19.1 %collective-permute-start = (bf16[128,256]{1,0:T(8,128)(2,1)S(1)}, bf16[128,256]{1,0:T(8,128)(2,1)S(1)}, u32[]{:S(2)}, u32[]{:S(2)}) collective-permute-start(bf16[128,256]{1,0:T(8,128)(2,1)S(1)} %copy.95), channel_id=1, source_target_pairs={{0,1},{1,2},{2,3},{3,4},{4,5},{5,6},{6,7},{7,8},{8,9},{9,10},{10,1... | collective-permute-start | bytes 196616 | tf_op jit(solution)/shard_map/while/body/eval_jaxpr/ppermute | solution.py:16
  729.9 16.9 collective-permute-start.1
  748.3 21.5 %collective-permute-start.1 = (bf16[128,256]{1,0:T(8,128)(2,1)S(1)}, bf16[128,256]{1,0:T(8,128)(2,1)S(1)}, u32[]{:S(2)}, u32[]{:S(2)}) collective-permute-start(bf16[128,256]{1,0:T(8,128)(2,1)S(1)} %copy.116), channel_id=1, source_target_pairs={{0,63},{1,0},{2,1},{3,2},{4,3},{5,4},{6,5},{7,6},{8,7},{9,8},{10,9... | collective-permute-start | bytes 196616 | tf_op jit(solution)/shard_map/while/body/eval_jaxpr/ppermute | solution.py:16
  773.4 14.8 collective-permute-start.1
  791.6 16.7 collective-permute-start.1
  810.3 15.9 collective-permute-start.1
  828.8 16.3 collective-permute-start.1
  954.6 15.7 collective-permute-start.1
  972.3 16.4 collective-permute-start.1
  990.7 15.5 collective-permute-start.1
  1026.1 15.3 collective-permute-start.1
  1043.4 15.0 collective-permute-start.1
  1061.5 15.6 collective-permute-start.1
  1079.4 16.2 collective-permute-start.1
  1097.7 14.8 collective-permute-start.1
  1132.2 15.9 collective-permute-start.1
  1150.3 14.8 collective-permute-start.1
  1168.5 15.6 collective-permute-start.1
  1186.3 15.6 collective-permute-start.1
  1221.9 15.3 collective-permute-start.1
  1238.8 16.6 collective-permute-start.1
  1257.1 15.7 collective-permute-start.1
  1275.3 15.1 collective-permute-start.1
  1293.2 15.5 collective-permute-start.1
  1310.8 14.7 collective-permute-start.1
  1345.8 15.7 collective-permute-start.1
  1363.8 15.7 collective-permute-start.1
  1381.9 15.0 collective-permute-start.1
  1399.9 15.4 collective-permute-start.1
  1417.3 14.8 collective-permute-start.1
  1435.4 14.8 collective-permute-start.1
  1452.5 15.8 collective-permute-start.1
  1470.6 15.4 collective-permute-start.1
  1488.6 14.9 collective-permute-start.1
  1505.9 16.0 collective-permute-start.1
  1524.1 14.8 collective-permute-start.1
  1558.8 15.7 collective-permute-start.1
  1576.9 15.6 collective-permute-start.1
  1594.3 16.5 collective-permute-start.1
  1612.9 15.5 collective-permute-start.1
  1664.8 16.0 collective-permute-start.1
  1682.5 16.9 collective-permute-start.1
  1701.6 16.0 collective-permute-start.1
  1754.1 16.0 collective-permute-start.1
  1772.2 15.5 collective-permute-start.1
  1790.4 15.8 collective-permute-start.1
  1807.7 16.1 collective-permute-start.1
  (276 other events, 1377.3 us)
where the time goes:
time: 1860 us; the launch traced here: 1830 us
  starting transfers between devices  827 us (44%)
  waiting for transfers between devices  567 us (30%)
  matrix products  192 us (10%)
  local copies, waits for them, and re-layouts  189 us (10%)
  other arithmetic  38.8 us (2%)
    ppermute x189, starting transfers between devices, passed_along(): lax.ppermute(x, axis, [(i, (i + by) % length) for i in range(length)])  813 us
    ppermute x189, waiting for transfers between devices, passed_along(): lax.ppermute(x, axis, [(i, (i + by) % length) for i in range(length)])  550 us
    dynamic_slice x64, local copies, waits for them, and re-layouts, visit(): lax.dynamic_slice_in_dim(positions, block_index * rows_here, rows_here)  48.7 us
    dynamic_slice x63, local copies, waits for them, and re-layouts, backward_block(): lax.dynamic_slice_in_dim(positions, block_index * rows_here, rows_here)  47.8 us
    while x378, local copies, waits for them, and re-layouts  40.6 us
    dot_general x128, matrix products, forward_tile(): jnp.einsum('grqk,kgd->grqd', weights, value_rows.astype(jnp.float32), pre...  38.9 us
  transfers between devices with their start and end apart: 192, of which 129 were waited for; matrix products, arithmetic and copies ran while one was open for 18% of the time, Pallas kernels for 0%

commit v1 on v0

v1 whole, which is shorter than its diff:
```python
import jax
import jax.numpy as jnp
from jax import lax
from jax.experimental import pallas as pl
from jax.experimental.pallas import tpu as pltpu
from jax.sharding import PartitionSpec as P

QH = 32
KVH = 8
DH = 128
RUN = 64
BLOCKS = 64
RATIO = QH // KVH
ROWS = RATIO * RUN
CHUNK = 256
RUNS_CHUNK = CHUNK // RUN
CHUNKS = 2 * BLOCKS // RUNS_CHUNK
ITEMS = CHUNKS + 1
LOG2E = 1.4426950408889634
SCALE = DH**-0.5
NEG_FILL = -1e30
F32 = jnp.float32
BF16 = jnp.bfloat16


def dot(a, b, ca, cb):
    return lax.dot_general(a, b, (((ca,), (cb,)), ((), ())), preferred_element_type=F32)


def attention_kernel(
    own_ref,
    pb_ref,
    q_ref,
    do_ref,
    kv_ref,
    out_ref,
    dq_ref,
    dkv_ref,
    loc,
    qs,
    dos,
    kvs,
    kvt,
    scores,
    probs,
    dkvs,
    top,
    total,
    acc_out,
    acc_dq,
    qd,
    dod,
    delta,
):
    own = pb_ref[own_ref[0]]
    first_chunks = own // RUNS_CHUNK

    def place(b, carry):
        p = pb_ref[b]
        loc[p] = 2 * b
        loc[2 * BLOCKS - 1 - p] = 2 * b + 1
        return carry

    lax.fori_loop(0, BLOCKS, place, 0)

    for s in range(2):
        rows = slice(s * RUN, (s + 1) * RUN)
        for h in range(RATIO):
            cols = slice(h * DH, (h + 1) * DH)
            qs[s, h * RUN : (h + 1) * RUN, :] = q_ref[rows, cols]
            dos[s, h * RUN : (h + 1) * RUN, :] = do_ref[rows, cols]

    def sort_chunk(c, carry):
        for j in range(RUNS_CHUNK):
            start = pl.multiple_of(loc[c * RUNS_CHUNK + j] * RUN, RUN)
            kvs[c, j * RUN : (j + 1) * RUN, :] = kv_ref[pl.ds(start, RUN), :]
        kvt[c] = kvs[c].T
        dkvs[c] = jnp.zeros((CHUNK, 2 * DH), F32)
        return carry

    lax.fori_loop(0, CHUNKS, sort_chunk, 0)

    top[...] = jnp.full(top.shape, NEG_FILL, F32)
    total[...] = jnp.zeros(total.shape, F32)
    acc_out[...] = jnp.zeros(acc_out.shape, F32)
    acc_dq[...] = jnp.zeros(acc_dq.shape, F32)

    def item(t):
        late = t >= first_chunks
        sel = jnp.where(late, 1, 0)
        return sel, jnp.where(late, t - first_chunks, t)

    def sweep(visit):
        def some(i, carry):
            for j in range(3):
                t = 3 * i + j
                sel, c = item(t)
                visit(t, sel, c, None)
            return carry

        lax.fori_loop(0, (ITEMS - 3) // 3, some, 0)
        sel, c = item(ITEMS - 3)
        visit(ITEMS - 3, sel, c, None)
        visit(ITEMS - 2, 0, first_chunks, own * RUN)
        visit(ITEMS - 1, 1, CHUNKS - 1 - first_chunks, (2 * BLOCKS - 1 - own) * RUN)

    def fold(x, op):
        return op(x.reshape(CHUNK // 8, 8, ROWS), axis=0)

    def score(t, sel, c, first_pos):
        s = dot(kvs[c, :, :DH], qs[sel], 1, 1)
        if first_pos is not None:
            key = c * CHUNK + lax.broadcasted_iota(jnp.int32, (CHUNK, ROWS), 0)
            row = first_pos + lax.rem(lax.broadcasted_iota(jnp.int32, (CHUNK, ROWS), 1), RUN)
            s = jnp.where(key <= row, s, NEG_FILL)
        scores[t] = s
        top[sel] = jnp.maximum(top[sel], fold(s, jnp.max))

    sweep(score)
    for s in range(2):
        m = jnp.max(top[s], axis=0, keepdims=True) * (SCALE * LOG2E)
        top[s] = jnp.broadcast_to(m, (8, ROWS))

    def weigh(t, sel, c, first_pos):
        e = jnp.exp2(scores[t] * (SCALE * LOG2E) - top[sel, 0:1, :])
        total[sel] += fold(e, jnp.sum)
        e = e.astype(BF16)
        probs[t] = e
        acc_out[sel] += dot(kvt[c, DH:, :], e, 1, 0)

    sweep(weigh)
    for s in range(2):
        inv = 1.0 / jnp.sum(total[s], axis=0, keepdims=True)
        out = (acc_out[s] * inv).astype(BF16).astype(F32)
        d_rows = dos[s].astype(F32)
        delta[s] = jnp.broadcast_to(jnp.sum(out * d_rows.T, axis=0, keepdims=True), (8, ROWS))
        total[s] = jnp.broadcast_to(inv, (8, ROWS))
        inv_rows = jnp.broadcast_to(inv, (DH, ROWS)).T
        dod[s] = (d_rows * inv_rows).astype(BF16)
        qd[s] = (qs[s].astype(F32) * (inv_rows * SCALE)).astype(BF16)
        out = out.T.astype(BF16)
        for h in range(RATIO):
            out_ref[s * RUN : (s + 1) * RUN, h * DH : (h + 1) * DH] = out[h * RUN : (h + 1) * RUN]

    def backward(t, sel, c, first_pos):
        e = probs[t]
        dp = dot(kvs[c, :, DH:], dos[sel], 1, 1)
        ds = (e.astype(F32) * (dp - delta[sel, 0:1, :])).astype(BF16)
        dkvs[c, :, DH:] += dot(e, dod[sel], 1, 0)
        dkvs[c, :, :DH] += dot(ds, qd[sel], 1, 0)
        acc_dq[sel] += dot(kvt[c, :DH, :], ds, 1, 0)

    sweep(backward)
    for s in range(2):
        grad = (acc_dq[s] * (total[s, 0:1, :] * SCALE)).T.astype(BF16)
        for h in range(RATIO):
            dq_ref[s * RUN : (s + 1) * RUN, h * DH : (h + 1) * DH] = grad[h * RUN : (h + 1) * RUN]

    def unsort_chunk(c, carry):
        for j in range(RUNS_CHUNK):
            start = pl.multiple_of(loc[c * RUNS_CHUNK + j] * RUN, RUN)
            dkv_ref[pl.ds(start, RUN), :] = dkvs[c, j * RUN : (j + 1) * RUN, :].astype(BF16)
        return carry

    lax.fori_loop(0, CHUNKS, unsort_chunk, 0)


def attention(own, pb, q, do, kv):
    rows, width = q.shape
    vmem = pl.BlockSpec(memory_space=pltpu.VMEM)
    smem = pl.BlockSpec(memory_space=pltpu.SMEM)
    return pl.pallas_call(
        attention_kernel,
        out_shape=(
            jax.ShapeDtypeStruct((rows, width), BF16),
            jax.ShapeDtypeStruct((rows, width), BF16),
            jax.ShapeDtypeStruct(kv.shape, BF16),
        ),
        in_specs=[smem, smem, vmem, vmem, vmem],
        out_specs=(vmem, vmem, vmem),
        scratch_shapes=[
            pltpu.SMEM((2 * BLOCKS,), jnp.int32),
            pltpu.VMEM((2, ROWS, DH), BF16),
            pltpu.VMEM((2, ROWS, DH), BF16),
            pltpu.VMEM((CHUNKS, CHUNK, 2 * DH), BF16),
            pltpu.VMEM((CHUNKS, 2 * DH, CHUNK), BF16),
            pltpu.VMEM((ITEMS, CHUNK, ROWS), F32),
            pltpu.VMEM((ITEMS, CHUNK, ROWS), BF16),
            pltpu.VMEM((CHUNKS, CHUNK, 2 * DH), F32),
            pltpu.VMEM((2, 8, ROWS), F32),
            pltpu.VMEM((2, 8, ROWS), F32),
            pltpu.VMEM((2, DH, ROWS), F32),
            pltpu.VMEM((2, DH, ROWS), F32),
            pltpu.VMEM((2, ROWS, DH), BF16),
            pltpu.VMEM((2, ROWS, DH), BF16),
            pltpu.VMEM((2, 8, ROWS), F32),
        ],
        compiler_params=pltpu.CompilerParams(vmem_limit_bytes=56 * 1024 * 1024),
    )(own, pb, q, do, kv)


def shards(q_rows, k_rows, v_rows, dout, positions):
    heads = lax.axis_size("head")
    tokens = q_rows.shape[0]
    q_width = q_rows.shape[1] // heads
    kv_width = k_rows.shape[1] // heads
    mixed = jnp.concatenate(
        [
            q_rows.reshape(tokens, heads, q_width),
            k_rows.reshape(tokens, heads, kv_width),
            v_rows.reshape(tokens, heads, kv_width),
        ],
        axis=2,
    )
    mine = lax.all_to_all(mixed, "head", split_axis=1, concat_axis=0, tiled=True)
    mine = mine.reshape(heads * tokens, q_width + 2 * kv_width)
    kv = lax.all_gather(mine[:, q_width:], ("inner", "outer"), axis=0, tiled=True)
    own = lax.axis_index("inner") * lax.axis_size("outer") + lax.axis_index("outer")
    pb = positions[:: 2 * RUN] // RUN
    attn_out, grad_q, dkv = attention(own.reshape(1), pb, mine[:, :q_width], dout, kv)
    dkv = lax.psum_scatter(dkv, ("inner", "outer"), scatter_dimension=0, tiled=True)
    return attn_out, grad_q, dkv[:, :kv_width], dkv[:, kv_width:]


def solution(mesh):
    return jax.shard_map(
        shards,
        mesh=mesh,
        in_specs=(
            P(("inner", "outer", "head"), None),
            P(("inner", "outer", "head"), None),
            P(("inner", "outer", "head"), None),
            P(("inner", "outer"), "head"),
            P(),
        ),
        out_specs=(
            P(("inner", "outer"), "head"),
            P(("inner", "outer"), "head"),
            P(("inner", "outer"), "head"),
            P(("inner", "outer"), "head"),
        ),
        check_vma=False,
    )
```

time: 1860 us -> 579 us (0.31)
  the two profiles are of different devices: /device:TPU:1 before, /device:TPU:88 now
where the time goes in v1:
time: 579 us
  waiting for transfers between devices  521 us (90%)
  Pallas kernels  24 us (4%)
  blocking collectives  14.2 us (2%)
  between operations  14.1 us (2%)
    reduce_scatter x1, waiting for transfers between devices, shards(): lax.psum_scatter(dkv, ('inner', 'outer'), scatter_dimension=0, tiled=True)  328 us
    all_gather x1, waiting for transfers between devices, shards(): lax.all_gather(mine[:, q_width:], ('inner', 'outer'), axis=0, tiled=True)  192 us
    pallas_call x1, Pallas kernels, attention(): pl.pallas_call(attention_kernel, out_shape=(jax.ShapeDtypeStruct((rows, w...  24 us
    all_to_all x1, blocking collectives, shards(): lax.all_to_all(mixed, 'head', split_axis=1, concat_axis=0, tiled=True)  14.2 us
  transfers between devices with their start and end apart: 2, of which 2 were waited for; matrix products, arithmetic and copies ran while one was open for 0% of the time, Pallas kernels for 0%

profile of v1, /device:TPU:88, one launch (start us, length us, event | category | flops | bytes accessed | tf_op | source)
XLA Modules:
  0.0 578.9 jit_solution(578293984936618395)
XLA Ops:
  7.2 0.0 copy-start
  7.2 0.0 all-gather.2.cloned.1.call-start
  7.2 0.9 copy.18
  8.1 0.0 copy-done
  8.2 0.8 copy_bitcast_fusion.1
  9.0 14.2 %all_to_all.15 = bf16[16,8,768]{2,0,1:T(8,128)(2,1)S(1)} all-to-all(bf16[16,8,768]{2,0,1:T(8,128)(2,1)S(1)} %pad_maximum_fusion), channel_id=1, replica_groups=mesh['head'=8,'inner'=4,'outer'=16] {'head'}, dimensions={1} | all-to-all | bytes 393216 | tf_op jit(solution)/shard_map/all_to_all | solution.py:215
  23.1 0.6 slice.21
  23.8 0.0 all-gather.2.cloned.1.call-update
  23.8 0.0 reduce-scatter.2.cloned.1.call-start
  23.9 0.9 slice.15
  24.8 0.5 and_select_fusion.pb_ref
  25.3 0.6 slice.20.q_ref
  25.9 192.5 %all-gather.2.cloned.1.call-done.kv_ref = bf16[8192,256]{1,0:T(8,128)(2,1)} async-done(((bf16[128,256]{1,0:T(8,128)(2,1)}), bf16[8192,256]{1,0:T(8,128)(2,1)}) %all-gather.2.cloned.1.call-update) | async-done | bytes 4194320 | tf_op jit(solution)/shard_map/all_gather | solution.py:217
  218.4 24.0 %shard_map.84 = (bf16[128,512]{1,0:T(8,128)(2,1)}, bf16[128,512]{1,0:T(8,128)(2,1)}, bf16[8192,256]{1,0:T(8,128)(2,1)}) custom-call(s32[1]{0:T(128)} %bitcast.own_ref, s32[64]{0:T(128)} %and_select_fusion.pb_ref, bf16[128,512]{1,0:T(8,128)(2,1)} %slice.20.q_ref, bf16[128,512]{1,0:T(8,128)(2,1)} %do_ref.1, bf16[8192,256]{1,0:T(8,128)(2,1)} %all-gather.2.cloned.1.call-done.kv_ref), custom_call_target="tpu_custom_call" | custom-call | tf_op jit(solution)/shard_map/pallas_call | solution.py:172
  242.4 0.0 reduce-scatter.2.cloned.1.call-update
  242.5 328.2 %reduce-scatter.2.cloned.1.call-done = bf16[128,256]{1,0:T(8,128)(2,1)} async-done(((bf16[8192,256]{1,0:T(8,128)(2,1)}), bf16[128,256]{1,0:T(8,128)(2,1)}) %reduce-scatter.2.cloned.1.call-update) | async-done | bytes 65552 | tf_op jit(solution)/shard_map/reduce_scatter | solution.py:221
  570.6 1.4 fusion
  (1 shorter events, 0.0 us)
Async XLA Ops:
  7.2 1.0 copy-start
  7.2 211.2 %all-gather.2.cloned.1.call-start = ((), (), s32[]{:S(2)}) async-start(), calls=%async_computation.2 | async-start | bytes 4259840 | tf_op jit(solution)/shard_map/all_gather | solution.py:217
  23.8 546.8 %reduce-scatter.2.cloned.1.call-start = ((), (), s32[]{:S(2)}) async-start(), calls=%async_computation.3 | async-start | bytes 4259840 | tf_op jit(solution)/shard_map/reduce_scatter | solution.py:221
Sparse Core Ops, SparseCore 0:
  23.9 194.4 all-gather.1
  242.6 328.0 reduce-scatter.1

commit v2 on v1

--- a/solution.py
+++ b/solution.py
@@ -1,3 +1,5 @@
+import functools
+
 import jax
 import jax.numpy as jnp
 from jax import lax
@@ -10,6 +12,7 @@
 DH = 128
 RUN = 64
 BLOCKS = 64
+CHIPS_X = 4
 RATIO = QH // KVH
 ROWS = RATIO * RUN
 CHUNK = 256
@@ -199,6 +202,276 @@
     )(own, pb, q, do, kv)
 
 
+MESH = pl.DeviceIdType.MESH
+
+
+class Plane:
+    def __init__(self, x_count):
+        inner, outer = lax.axis_index("inner"), lax.axis_index("outer")
+        self.xs = x_count
+        self.z_pairs = lax.axis_size("outer") // x_count
+        self.zs = 2 * self.z_pairs
+        self.x = lax.rem(outer, x_count)
+        self.core = lax.rem(inner, 2)
+        self.z = 2 * lax.div(outer, x_count) + lax.div(inner, 2)
+
+    def z_off(self, by):
+        return lax.rem(self.z + by + self.zs, self.zs)
+
+    def x_off(self, by):
+        return lax.rem(self.x + by + self.xs, self.xs)
+
+    def group(self, z, core):
+        return (2 * lax.rem(z, 2) + core) * self.z_pairs + lax.div(z, 2)
+
+    def device(self, z=None, core=None, x=None):
+        z = self.z if z is None else z
+        core = self.core if core is None else core
+        x = self.x if x is None else x
+        return {"inner": 2 * lax.rem(z, 2) + core, "outer": lax.div(z, 2) * self.xs + x}
+
+    def partners(self):
+        found = [self.device(core=1 - self.core)]
+        found += [self.device(z=self.z_off(1)), self.device(z=self.z_off(-1))]
+        found += [self.device(x=self.x_off(d)) for d in range(1, self.xs)]
+        return found
+
+    def greet(self):
+        barrier = pltpu.get_barrier_semaphore()
+        partners = self.partners()
+        for device in partners:
+            pl.semaphore_signal(barrier, inc=1, device_id=device, device_id_type=MESH)
+        pl.semaphore_wait(barrier, len(partners))
+
+
+def push(src, dst, send_sem, recv_sem, device):
+    copy = pltpu.make_async_remote_copy(
+        src_ref=src,
+        dst_ref=dst,
+        send_sem=send_sem,
+        recv_sem=recv_sem,
+        device_id=device,
+        device_id_type=MESH,
+    )
+    copy.start()
+    return copy
+
+
+def gather_kernel(
+    x_count, own_ref, out_ref, own_sem, x_send, x_recv, z_send, z_recv, c_send, c_recv
+):
+    at = Plane(x_count)
+    far = at.zs // 2
+    rows = own_ref.shape[0]
+    group_rows = out_ref.shape[1]
+    half_rows = group_rows // 2
+    at.greet()
+
+    group = at.group(at.z, at.core)
+    slot = out_ref.at[group, pl.ds(pl.multiple_of(at.x * rows, rows), rows), :]
+    own = pltpu.make_async_copy(own_ref, slot, own_sem)
+    own.start()
+    sent = [
+        push(own_ref, slot, x_send.at[d - 1], x_recv.at[d - 1], at.device(x=at.x_off(d)))
+        for d in range(1, at.xs)
+    ]
+    own.wait()
+    for copy in sent:
+        copy.wait_recv()
+
+    crossed = []
+
+    def cross(group):
+        i = len(crossed)
+        whole = out_ref.at[group]
+        crossed.append(
+            push(whole, whole, c_send.at[i], c_recv.at[i], at.device(core=1 - at.core))
+        )
+
+    def along(way, step, group):
+        if step == far - 1:
+            part = out_ref.at[group, pl.ds(way * half_rows, half_rows), :]
+        else:
+            part = out_ref.at[group]
+        target = at.device(z=at.z_off(1 - 2 * way))
+        return push(part, part, z_send.at[way, step], z_recv.at[way, step], target)
+
+    moving = [along(way, 0, group) for way in range(2)]
+    cross(group)
+    for step in range(far):
+        for way in range(2):
+            moving[way].wait_recv()
+            sent.append(moving[way])
+            group = at.group(at.z_off((2 * way - 1) * (step + 1)), at.core)
+            if step < far - 1:
+                moving[way] = along(way, step + 1, group)
+                cross(group)
+    cross(group)
+    for copy in crossed:
+        copy.wait_recv()
+    for copy in sent + crossed:
+        copy.wait_send()
+
+
+def gather(x_count, kv):
+    rows, width = kv.shape
+    z_pairs = lax.axis_size("outer") // x_count
+    zs = 2 * z_pairs
+    dma = pltpu.SemaphoreType.DMA
+    return pl.pallas_call(
+        functools.partial(gather_kernel, x_count),
+        out_shape=jax.ShapeDtypeStruct((2 * zs, x_count * rows, width), kv.dtype),
+        in_specs=[pl.BlockSpec(memory_space=pltpu.VMEM)],
+        out_specs=pl.BlockSpec(memory_space=pl.ANY),
+        scratch_shapes=[
+            dma,
+            dma((x_count - 1,)),
+            dma((x_count - 1,)),
+            dma((2, zs // 2)),
+            dma((2, zs // 2)),
+            dma((zs,)),
+            dma((zs,)),
+        ],
+        compiler_params=pltpu.CompilerParams(collective_id=0, has_side_effects=True),
+    )(kv)
+
+
+def scatter_kernel(
+    x_count,
+    part_ref,
+    gk_ref,
+    gv_ref,
+    other,
+    held,
+    sums,
+    total,
+    x_out,
+    x_in,
+    x_send,
+    x_recv,
+    z_send,
+    z_recv,
+    c_send,
+    c_recv,
+):
+    at = Plane(x_count)
+    far = at.zs // 2
+    group_rows = part_ref.shape[1]
+    half_rows = group_rows // 2
+    rows = gk_ref.shape[0]
+    at.greet()
+
+    offsets = [far]
+    for step in range(1, far):
+        offsets += [far - step, step - far]
+    offsets.append(0)
+    crossed = [
+        push(
+            part_ref.at[at.group(at.z_off(offset), 1 - at.core)],
+            other.at[i],
+            c_send.at[i],
+            c_recv.at[i],
+            at.device(core=1 - at.core),
+        )
+        for i, offset in enumerate(offsets)
+    ]
+
+    def pair(i):
+        crossed[i].wait_recv()
+        mine = part_ref[at.group(at.z_off(offsets[i]), at.core)]
+        return mine.astype(F32) + other[i].astype(F32)
+
+    def along(way, step):
+        place = pl.ds(way * half_rows, half_rows) if step == 0 else pl.ds(0, group_rows)
+        return push(
+            sums.at[way, step, place, :],
+            held.at[way, step, place, :],
+            z_send.at[way, step],
+            z_recv.at[way, step],
+            at.device(z=at.z_off(1 - 2 * way)),
+        )
+
+    sent = []
+    start = pair(0).astype(BF16)
+    moving = []
+    for way in range(2):
+        place = slice(way * half_rows, (way + 1) * half_rows)
+        sums[way, 0, place, :] = start[place]
+        moving.append(along(way, 0))
+    for step in range(1, far):
+        for way in range(2):
+            mine = pair(2 * step - 1 + way)
+            moving[way].wait_recv()
+            sent.append(moving[way])
+            if step == 1:
+                place = slice(way * half_rows, (way + 1) * half_rows)
+                rest = slice((1 - way) * half_rows, (2 - way) * half_rows)
+                arrived = held[way, 0, place, :].astype(F32)
+                sums[way, 1, place, :] = (mine[place] + arrived).astype(BF16)
+                sums[way, 1, rest, :] = mine[rest].astype(BF16)
+            else:
+                sums[way, step] = (mine + held[way, step - 1].astype(F32)).astype(BF16)
+            moving[way] = along(way, step)
+    mine = pair(at.zs - 1)
+    for way in range(2):
+        moving[way].wait_recv()
+        sent.append(moving[way])
+        mine = mine + held[way, far - 1].astype(F32)
+    total[...] = mine
+    x_out[...] = mine.astype(BF16)
+    across = []
+    for d in range(1, at.xs):
+        x = at.x_off(d)
+        across.append(
+            push(
+                x_out.at[pl.ds(pl.multiple_of(x * rows, rows), rows), :],
+                x_in.at[d - 1],
+                x_send.at[d - 1],
+                x_recv.at[d - 1],
+                at.device(x=x),
+            )
+        )
+    result = total[pl.ds(pl.multiple_of(at.x * rows, rows), rows), :]
+    for d in range(1, at.xs):
+        across[d - 1].wait_recv()
+        result = result + x_in[d - 1].astype(F32)
+    gk_ref[...] = result[:, :DH].astype(BF16)
+    gv_ref[...] = result[:, DH:].astype(BF16)
+    for copy in sent + crossed + across:
+        copy.wait_send()
+
+
+def scatter(x_count, parts):
+    groups, group_rows, width = parts.shape
+    rows = group_rows // x_count
+    far = groups // 4
+    vmem = pl.BlockSpec(memory_space=pltpu.VMEM)
+    dma = pltpu.SemaphoreType.DMA
+    return pl.pallas_call(
+        functools.partial(scatter_kernel, x_count),
+        out_shape=(jax.ShapeDtypeStruct((rows, DH), BF16),) * 2,
+        in_specs=[vmem],
+        out_specs=(vmem, vmem),
+        scratch_shapes=[
+            pltpu.VMEM((2 * far, group_rows, width), BF16),
+            pltpu.VMEM((2, far, group_rows, width), BF16),
+            pltpu.VMEM((2, far, group_rows, width), BF16),
+            pltpu.VMEM((group_rows, width), F32),
+            pltpu.VMEM((group_rows, width), BF16),
+            pltpu.VMEM((x_count - 1, rows, width), BF16),
+            dma((x_count - 1,)),
+            dma((x_count - 1,)),
+            dma((2, far)),
+            dma((2, far)),
+            dma((2 * far,)),
+            dma((2 * far,)),
+        ],
+        compiler_params=pltpu.CompilerParams(
+            collective_id=1, has_side_effects=True, vmem_limit_bytes=32 * 1024 * 1024
+        ),
+    )(parts)
+
+
 def shards(q_rows, k_rows, v_rows, dout, positions):
     heads = lax.axis_size("head")
     tokens = q_rows.shape[0]
@@ -214,12 +487,13 @@
     )
     mine = lax.all_to_all(mixed, "head", split_axis=1, concat_axis=0, tiled=True)
     mine = mine.reshape(heads * tokens, q_width + 2 * kv_width)
-    kv = lax.all_gather(mine[:, q_width:], ("inner", "outer"), axis=0, tiled=True)
+    kv = gather(CHIPS_X, mine[:, q_width:])
     own = lax.axis_index("inner") * lax.axis_size("outer") + lax.axis_index("outer")
     pb = positions[:: 2 * RUN] // RUN
-    attn_out, grad_q, dkv = attention(own.reshape(1), pb, mine[:, :q_width], dout, kv)
-    dkv = lax.psum_scatter(dkv, ("inner", "outer"), scatter_dimension=0, tiled=True)
-    return attn_out, grad_q, dkv[:, :kv_width], dkv[:, kv_width:]
+    kv_flat = kv.reshape(-1, 2 * kv_width)
+    attn_out, grad_q, dkv = attention(own.reshape(1), pb, mine[:, :q_width], dout, kv_flat)
+    grad_k, grad_v = scatter(CHIPS_X, dkv.reshape(kv.shape))
+    return attn_out, grad_q, grad_k, grad_v
 
 
 def solution(mesh):

time: 579 us -> 130 us (0.22)
  the two profiles are of different devices: /device:TPU:88 before, /device:TPU:1 now
where the time goes in v2:
time: 130 us; the launch traced here: 129 us
  Pallas kernels  104 us (80%)
  starting transfers between devices  7.65 us (6%)
  local copies, waits for them, and re-layouts  7.31 us (6%)
  waiting for transfers between devices  7.31 us (6%)
    pallas_call x1, Pallas kernels, gather(): pl.pallas_call(functools.partial(gather_kernel, x_count), out_shape=jax.S...  46.5 us
    pallas_call x1, Pallas kernels, scatter(): pl.pallas_call(functools.partial(scatter_kernel, x_count), out_shape=(jax...  33.8 us
    pallas_call x1, Pallas kernels, attention(): pl.pallas_call(attention_kernel, out_shape=(jax.ShapeDtypeStruct((rows, w...  24.1 us
    all_to_all x1, starting transfers between devices, shards(): lax.all_to_all(mixed, 'head', split_axis=1, concat_axis=0, tiled=True)  7.65 us
    all_to_all x1, waiting for transfers between devices, shards(): lax.all_to_all(mixed, 'head', split_axis=1, concat_axis=0, tiled=True)  7.31 us
    unnamed x6, local copies, waits for them, and re-layouts  3.43 us
  transfers between devices with their start and end apart: 1, of which 1 were waited for; matrix products, arithmetic and copies ran while one was open for 1% of the time, Pallas kernels for 0%

profile of v2, /device:TPU:1, one launch (start us, length us, event | category | flops | bytes accessed | tf_op | source)
XLA Modules:
  0.0 128.5 jit_solution(9354596815991842513)
XLA Ops:
  0.6 0.0 copy-start
  0.6 0.9 copy.18
  1.6 0.0 copy-done
  1.6 0.8 copy_bitcast_fusion.1
  2.4 0.7 pad_maximum_fusion
  3.0 7.7 %all-to-all-start = ((bf16[16,8,768]{2,0,1:T(8,128)(2,1)}), bf16[16,8,768]{2,0,1:T(8,128)(2,1)S(1)}, u32[]{:S(2)}, u32[]{:S(2)}) async-start(bf16[16,8,768]{2,0,1:T(8,128)(2,1)} %pad_maximum_fusion), calls=%async_computation | async-start | bytes 393216 | tf_op jit(solution)/shard_map/all_to_all | solution.py:488
  10.7 0.9 slice.9
  11.6 0.5 and_select_fusion.pb_ref
  12.1 7.3 %all-to-all-done = bf16[16,8,768]{2,0,1:T(8,128)(2,1)S(1)} async-done(((bf16[16,8,768]{2,0,1:T(8,128)(2,1)}), bf16[16,8,768]{2,0,1:T(8,128)(2,1)S(1)}, u32[]{:S(2)}, u32[]{:S(2)}) %all-to-all-start) | async-done | bytes 196640 | tf_op jit(solution)/shard_map/all_to_all | solution.py:488
  19.4 0.6 slice.13.own_ref
  20.1 0.7 slice.12.q_ref
  20.7 46.5 %shard_map.84 = bf16[16,512,256]{2,1,0:T(8,128)(2,1)} custom-call(bf16[128,256]{1,0:T(8,128)(2,1)} %slice.13.own_ref), custom_call_target="tpu_custom_call" | custom-call | tf_op jit(solution)/shard_map/pallas_call | solution.py:321
  67.2 24.1 %shard_map.85 = (bf16[128,512]{1,0:T(8,128)(2,1)}, bf16[128,512]{1,0:T(8,128)(2,1)}, bf16[8192,256]{1,0:T(8,128)(2,1)}) custom-call(s32[1]{0:T(128)} %bitcast.own_ref, s32[64]{0:T(128)} %and_select_fusion.pb_ref, bf16[128,512]{1,0:T(8,128)(2,1)} %slice.12.q_ref, bf16[128,512]{1,0:T(8,128)(2,1)} %do_ref.1, bf16[8192,256]{1,0:T(8,128)(2,1)} %bitcast.23), custom_call_target="tpu_custom_call" | custom-call | tf_op jit(solution)/shard_map/pallas_call | solution.py:175
  91.3 0.0 copy-start.1
  91.3 2.2 %copy-done.1 = bf16[8192,256]{1,0:T(8,128)(2,1)S(1)} copy-done((bf16[8192,256]{1,0:T(8,128)(2,1)S(1)}, bf16[8192,256]{1,0:T(8,128)(2,1)}, u32[]{:S(2)}) %copy-start.1) | copy-done | bytes 4194328
  93.5 33.8 %shard_map.86 = (bf16[128,128]{1,0:T(8,128)(2,1)S(1)}, bf16[128,128]{1,0:T(8,128)(2,1)S(1)}) custom-call(bf16[16,512,256]{2,1,0:T(8,128)(2,1)S(1)} %bitcast.22), custom_call_target="tpu_custom_call" | custom-call | tf_op jit(solution)/shard_map/pallas_call | solution.py:450
  127.3 0.6 copy.21
  127.9 0.6 copy.22
Async XLA Ops:
  0.6 0.9 copy-start
  3.0 16.4 %all-to-all-start = ((bf16[16,8,768]{2,0,1:T(8,128)(2,1)}), bf16[16,8,768]{2,0,1:T(8,128)(2,1)S(1)}, u32[]{:S(2)}, u32[]{:S(2)}) async-start(bf16[16,8,768]{2,0,1:T(8,128)(2,1)} %pad_maximum_fusion), calls=%async_computation | async-start | bytes 393216 | tf_op jit(solution)/shard_map/all_to_all | solution.py:488
  91.3 2.2 %copy-start.1 = (bf16[8192,256]{1,0:T(8,128)(2,1)S(1)}, bf16[8192,256]{1,0:T(8,128)(2,1)}, u32[]{:S(2)}) copy-start(bf16[8192,256]{1,0:T(8,128)(2,1)} %get-tuple-element.11) | copy-start | bytes 12582916

commit v3 on v1

--- a/solution.py
+++ b/solution.py
@@ -1,3 +1,5 @@
+import functools
+
 import jax
 import jax.numpy as jnp
 from jax import lax
@@ -10,6 +12,7 @@
 DH = 128
 RUN = 64
 BLOCKS = 64
+CHIPS_X = 4
 RATIO = QH // KVH
 ROWS = RATIO * RUN
 CHUNK = 256
@@ -57,8 +60,8 @@
 
     def place(b, carry):
         p = pb_ref[b]
-        loc[p] = 2 * b
-        loc[2 * BLOCKS - 1 - p] = 2 * b + 1
+        loc[p] = b
+        loc[2 * BLOCKS - 1 - p] = BLOCKS + b
         return carry
 
     lax.fori_loop(0, BLOCKS, place, 0)
@@ -199,27 +202,467 @@
     )(own, pb, q, do, kv)
 
 
-def shards(q_rows, k_rows, v_rows, dout, positions):
+MESH = pl.DeviceIdType.MESH
+
+
+class Plane:
+    def __init__(self, x_count):
+        inner, outer = lax.axis_index("inner"), lax.axis_index("outer")
+        self.xs = x_count
+        self.z_pairs = lax.axis_size("outer") // x_count
+        self.zs = 2 * self.z_pairs
+        self.x = lax.rem(outer, x_count)
+        self.core = lax.rem(inner, 2)
+        self.z = 2 * lax.div(outer, x_count) + lax.div(inner, 2)
+
+    def z_off(self, by):
+        return lax.rem(self.z + by + self.zs, self.zs)
+
+    def x_off(self, by):
+        return lax.rem(self.x + by + self.xs, self.xs)
+
+    def group(self, z, core):
+        return (2 * lax.rem(z, 2) + core) * self.z_pairs + lax.div(z, 2)
+
+    def device(self, z=None, core=None, x=None):
+        z = self.z if z is None else z
+        core = self.core if core is None else core
+        x = self.x if x is None else x
+        return {"inner": 2 * lax.rem(z, 2) + core, "outer": lax.div(z, 2) * self.xs + x}
+
+    def partners(self):
+        found = [self.device(core=1 - self.core)]
+        found += [self.device(z=self.z_off(1)), self.device(z=self.z_off(-1))]
+        found += [self.device(x=self.x_off(d)) for d in range(1, self.xs)]
+        return found
+
+    def greet(self, heads=1):
+        head = lax.axis_index("head")
+        partners = [{"head": lax.rem(head + d, heads)} for d in range(1, heads)]
+        partners += self.partners()
+        barrier = pltpu.get_barrier_semaphore()
+        for device in partners:
+            pl.semaphore_signal(barrier, inc=1, device_id=device, device_id_type=MESH)
+        pl.semaphore_wait(barrier, len(partners))
+
+
+def push(src, dst, send_sem, recv_sem, device):
+    copy = pltpu.make_async_remote_copy(
+        src_ref=src,
+        dst_ref=dst,
+        send_sem=send_sem,
+        recv_sem=recv_sem,
+        device_id=device,
+        device_id_type=MESH,
+    )
+    copy.start()
+    return copy
+
+
+def gather_kernel(
+    x_count,
+    q_ref,
+    k_ref,
+    v_ref,
+    q_out,
+    out_ref,
+    q_got,
+    block,
+    own_sem,
+    y_send,
+    y_recv,
+    xa_send,
+    xa_recv,
+    za_send,
+    za_recv,
+    ca_send,
+    ca_recv,
+    xb_send,
+    xb_recv,
+    zb_send,
+    zb_recv,
+    cb_send,
+    cb_recv,
+):
+    at = Plane(x_count)
+    heads = lax.axis_size("head")
+    far = at.zs // 2
+    tokens = q_ref.shape[0]
+    width = q_ref.shape[1] // heads
+    rows = block.shape[0] // 2
+    at.greet(heads)
+
+    head = lax.axis_index("head")
+    here = pl.ds(pl.multiple_of(head * tokens, tokens), tokens)
+    q_moves, kv_moves = [], []
+    for d in range(1, heads):
+        peer = lax.rem(head + d, heads)
+        cols = pl.ds(pl.multiple_of(peer * DH, DH), DH)
+        for i, (src, dst) in enumerate(
+            (
+                (k_ref.at[:, cols], block.at[here, pl.ds(0, DH)]),
+                (v_ref.at[:, cols], block.at[here, pl.ds(DH, DH)]),
+            )
+        ):
+            kv_moves.append(
+                push(src, dst, y_send.at[i, d - 1], y_recv.at[i, d - 1], {"head": peer})
+            )
+    for d in range(1, heads):
+        peer = lax.rem(head + d, heads)
+        cols = pl.ds(pl.multiple_of(peer * width, width), width)
+        q_moves.append(
+            push(
+                q_ref.at[:, cols],
+                q_got.at[here, :],
+                y_send.at[2, d - 1],
+                y_recv.at[2, d - 1],
+                {"head": peer},
+            )
+        )
+    cols = pl.ds(pl.multiple_of(head * DH, DH), DH)
+    block[here, :DH] = k_ref[:, cols]
+    block[here, DH:] = v_ref[:, cols]
+    q_got[here, :] = q_ref[:, pl.ds(pl.multiple_of(head * width, width), width)]
+    for copy in kv_moves:
+        copy.wait_recv()
+    sent = kv_moves + q_moves
+
+    mine = pl.ds(pl.multiple_of(at.x * rows, rows), rows)
+    group = at.group(at.z, at.core)
+    runs = [block.at[pl.ds(half * rows, rows), :] for half in range(2)]
+    own = []
+    for half in range(2):
+        copy = pltpu.make_async_copy(runs[half], out_ref.at[half, group, mine, :], own_sem.at[half])
+        copy.start()
+        own.append(copy)
+
+    def across(src, dst, send, recv):
+        return [
+            push(src, dst, send.at[d - 1], recv.at[d - 1], at.device(x=at.x_off(d)))
+            for d in range(1, at.xs)
+        ]
+
+    def towards(way):
+        return at.device(z=at.z_off(1 - 2 * way))
+
+    def move_a(way, step, group):
+        size = x_count * rows
+        part = out_ref.at[0, group]
+        if step == far - 1:
+            part = out_ref.at[0, group, pl.ds(way * (size // 2), size // 2), :]
+        return push(part, part, za_send.at[way, step], za_recv.at[way, step], towards(way))
+
+    def move_b(way, step, group, src=None):
+        if step == far - 1:
+            place = pl.ds(pl.multiple_of(at.x * rows + way * (rows // 2), rows // 2), rows // 2)
+        else:
+            place = mine
+        part = out_ref.at[1, group, place, :]
+        src = part if src is None else src
+        return push(src, part, zb_send.at[way, step], zb_recv.at[way, step], towards(way))
+
+    crossed = []
+
+    def cross(half, i, group):
+        whole = out_ref.at[half, group]
+        send, recv = (cb_send, cb_recv) if half else (ca_send, ca_recv)
+        crossed.append(
+            push(whole, whole, send.at[i], recv.at[i], at.device(core=1 - at.core))
+        )
+
+    def spread_b(i, group):
+        part = out_ref.at[1, group, mine, :]
+        return group, i, across(part, part, xb_send.at[i], xb_recv.at[i])
+
+    def finish_b(spread):
+        group, i, copies = spread
+        for copy in copies:
+            copy.wait_recv()
+        sent.extend(copies)
+        cross(1, i, group)
+
+    first_a = across(runs[0], out_ref.at[0, group, mine, :], xa_send, xa_recv)
+    b_moves = [move_b(way, 0, group, runs[1]) for way in range(2)]
+    own[1].wait()
+    spreads = [spread_b(0, group)]
+    own[0].wait()
+    for copy in first_a:
+        copy.wait_recv()
+    sent += first_a
+    a_moves = [move_a(way, 0, group) for way in range(2)]
+    cross(0, 0, group)
+    for step in range(far):
+        groups = [at.group(at.z_off((2 * way - 1) * (step + 1)), at.core) for way in range(2)]
+        last = step == far - 1
+        fresh = []
+        for way in range(2):
+            b_moves[way].wait_recv()
+            sent.append(b_moves[way])
+            if not last:
+                b_moves[way] = move_b(way, step + 1, groups[way])
+                fresh.append(spread_b(2 * step + 1 + way, groups[way]))
+        if last:
+            fresh.append(spread_b(2 * far - 1, groups[0]))
+        for way in range(2):
+            a_moves[way].wait_recv()
+            sent.append(a_moves[way])
+            if not last:
+                a_moves[way] = move_a(way, step + 1, groups[way])
+                cross(0, 2 * step + 1 + way, groups[way])
+        if last:
+            cross(0, 2 * far - 1, groups[0])
+        for spread in spreads:
+            finish_b(spread)
+        spreads = fresh
+    for spread in spreads:
+        finish_b(spread)
+    for copy in q_moves:
+        copy.wait_recv()
+    q_out[...] = q_got[...]
+    for copy in crossed:
+        copy.wait_recv()
+    for copy in sent + crossed:
+        copy.wait_send()
+
+
+def gather(x_count, q_rows, k_rows, v_rows):
     heads = lax.axis_size("head")
     tokens = q_rows.shape[0]
-    q_width = q_rows.shape[1] // heads
-    kv_width = k_rows.shape[1] // heads
-    mixed = jnp.concatenate(
-        [
-            q_rows.reshape(tokens, heads, q_width),
-            k_rows.reshape(tokens, heads, kv_width),
-            v_rows.reshape(tokens, heads, kv_width),
-        ],
-        axis=2,
-    )
-    mine = lax.all_to_all(mixed, "head", split_axis=1, concat_axis=0, tiled=True)
-    mine = mine.reshape(heads * tokens, q_width + 2 * kv_width)
-    kv = lax.all_gather(mine[:, q_width:], ("inner", "outer"), axis=0, tiled=True)
+    rows = heads * tokens
+    width = q_rows.shape[1] // heads
+    z_pairs = lax.axis_size("outer") // x_count
+    zs = 2 * z_pairs
+    dma = pltpu.SemaphoreType.DMA
+    vmem = pl.BlockSpec(memory_space=pltpu.VMEM)
+    sems = [(2,), (3, heads - 1), (3, heads - 1)]
+    for x_dims in ((x_count - 1,), (zs, x_count - 1)):
+        sems += [x_dims, x_dims, (2, zs // 2), (2, zs // 2), (zs,), (zs,)]
+    return pl.pallas_call(
+        functools.partial(gather_kernel, x_count),
+        out_shape=(
+            jax.ShapeDtypeStruct((rows, width), BF16),
+            jax.ShapeDtypeStruct((2, 2 * zs, x_count * rows // 2, 2 * DH), BF16),
+        ),
+        in_specs=[vmem, vmem, vmem],
+        out_specs=(vmem, pl.BlockSpec(memory_space=pl.ANY)),
+        scratch_shapes=[
+            pltpu.VMEM((rows, width), BF16),
+            pltpu.VMEM((rows, 2 * DH), BF16),
+        ]
+        + [dma(dims) for dims in sems],
+        compiler_params=pltpu.CompilerParams(collective_id=0, has_side_effects=True),
+    )(q_rows, k_rows, v_rows)
+
+
+def scatter_kernel(
+    x_count,
+    part_ref,
+    gk_ref,
+    gv_ref,
+    other,
+    za_in,
+    za_out,
+    zb_in,
+    zb_out,
+    xa_in,
+    xa_out,
+    xb_in,
+    xb_out,
+    keep,
+    xa_send,
+    xa_recv,
+    za_send,
+    za_recv,
+    ca_send,
+    ca_recv,
+    xb_send,
+    xb_recv,
+    zb_send,
+    zb_recv,
+    cb_send,
+    cb_recv,
+):
+    at = Plane(x_count)
+    far = at.zs // 2
+    size = part_ref.shape[2]
+    rows = size // x_count
+    at.greet()
+
+    offsets = [far]
+    for step in range(1, far):
+        offsets += [far - step, step - far]
+    offsets.append(0)
+    crossed = [[], []]
+    for i, offset in enumerate(offsets):
+        for half in (1, 0):
+            send, recv = (cb_send, cb_recv) if half else (ca_send, ca_recv)
+            crossed[half].append(
+                push(
+                    part_ref.at[half, at.group(at.z_off(offset), 1 - at.core)],
+                    other.at[half, i],
+                    send.at[i],
+                    recv.at[i],
+                    at.device(core=1 - at.core),
+                )
+            )
+
+    def pair(half, i):
+        crossed[half][i].wait_recv()
+        mine = part_ref[half, at.group(at.z_off(offsets[i]), at.core)]
+        return mine.astype(F32) + other[half, i].astype(F32)
+
+    sent = []
+
+    def across(src, dst, send, recv):
+        copies = []
+        for d in range(1, at.xs):
+            x = at.x_off(d)
+            place = pl.ds(pl.multiple_of(x * rows, rows), rows)
+            copies.append(
+                push(src.at[place, :], dst.at[d - 1], send.at[d - 1], recv.at[d - 1], at.device(x=x))
+            )
+        sent.extend(copies)
+        return copies
+
+    mine = pl.ds(pl.multiple_of(at.x * rows, rows), rows)
+
+    def spread_b(i):
+        total = pair(1, i)
+        keep[1, i] = total
+        xb_out[i] = total.astype(BF16)
+        return across(xb_out.at[i], xb_in.at[i], xb_send.at[i], xb_recv.at[i])
+
+    def collect(copies, kept, arrived):
+        total = kept[mine, :]
+        for d in range(1, at.xs):
+            copies[d - 1].wait_recv()
+            total = total + arrived[d - 1].astype(F32)
+        return total
+
+    def halves(way, length):
+        return pl.ds(way * (length // 2), length // 2)
+
+    def along(out, arrive, send, recv, way, step):
+        length = out.shape[2]
+        place = halves(way, length) if step == 0 else pl.ds(0, length)
+        copy = push(
+            out.at[way, step, place, :],
+            arrive.at[way, step, place, :],
+            send.at[way, step],
+            recv.at[way, step],
+            at.device(z=at.z_off(1 - 2 * way)),
+        )
+        sent.append(copy)
+        return copy
+
+    def begin(total, out, arrive, send, recv):
+        moves = []
+        length = out.shape[2]
+        for way in range(2):
+            out[way, 0, halves(way, length), :] = total[
+                way * (length // 2) : (way + 1) * (length // 2)
+            ].astype(BF16)
+            moves.append(along(out, arrive, send, recv, way, 0))
+        return moves
+
+    def go_on(moves, way, step, total, out, arrive, send, recv):
+        length = out.shape[2]
+        moves[way].wait_recv()
+        if step == 1:
+            near, rest = way, 1 - way
+            part = total[near * (length // 2) : (near + 1) * (length // 2)]
+            part = part + arrive[way, 0, halves(near, length), :].astype(F32)
+            out[way, 1, halves(near, length), :] = part.astype(BF16)
+            out[way, 1, halves(rest, length), :] = total[
+                rest * (length // 2) : (rest + 1) * (length // 2)
+            ].astype(BF16)
+        else:
+            out[way, step] = (total + arrive[way, step - 1].astype(F32)).astype(BF16)
+        moves[way] = along(out, arrive, send, recv, way, step)
+
+    def end(moves, total, arrive):
+        for way in range(2):
+            moves[way].wait_recv()
+            total = total + arrive[way, far - 1].astype(F32)
+        return total
+
+    a_refs = (za_out, za_in, za_send, za_recv)
+    b_refs = (zb_out, zb_in, zb_send, zb_recv)
+    spreads = {0: spread_b(0)}
+    a_moves = begin(pair(0, 0), *a_refs)
+
+    def collect_b(i):
+        return collect(spreads[i], keep.at[1, i], xb_in.at[i])
+
+    b_moves = None
+    for step in range(1, far):
+        for way in range(2):
+            spreads[2 * step - 1 + way] = spread_b(2 * step - 1 + way)
+        if step == 1:
+            b_moves = begin(collect_b(0), *b_refs)
+        else:
+            for way in range(2):
+                go_on(b_moves, way, step - 1, collect_b(2 * step - 3 + way), *b_refs)
+        for way in range(2):
+            go_on(a_moves, way, step, pair(0, 2 * step - 1 + way), *a_refs)
+    spreads[at.zs - 1] = spread_b(at.zs - 1)
+    for way in range(2):
+        go_on(b_moves, way, far - 1, collect_b(2 * far - 3 + way), *b_refs)
+    total = end(a_moves, pair(0, at.zs - 1), za_in)
+    keep[0, 0] = total
+    xa_out[...] = total.astype(BF16)
+    last_a = across(xa_out, xa_in, xa_send, xa_recv)
+    second = end(b_moves, collect_b(at.zs - 1), zb_in)
+    gk_ref[rows:, :] = second[:, :DH].astype(BF16)
+    gv_ref[rows:, :] = second[:, DH:].astype(BF16)
+    first = collect(last_a, keep.at[0, 0], xa_in)
+    gk_ref[:rows, :] = first[:, :DH].astype(BF16)
+    gv_ref[:rows, :] = first[:, DH:].astype(BF16)
+    for copy in sent + crossed[0] + crossed[1]:
+        copy.wait_send()
+
+
+def scatter(x_count, parts):
+    _, groups, size, width = parts.shape
+    rows = size // x_count
+    zs = groups // 2
+    far = zs // 2
+    vmem = pl.BlockSpec(memory_space=pltpu.VMEM)
+    dma = pltpu.SemaphoreType.DMA
+    sems = []
+    for x_dims in ((x_count - 1,), (zs, x_count - 1)):
+        sems += [x_dims, x_dims, (2, far), (2, far), (zs,), (zs,)]
+    return pl.pallas_call(
+        functools.partial(scatter_kernel, x_count),
+        out_shape=(jax.ShapeDtypeStruct((2 * rows, DH), BF16),) * 2,
+        in_specs=[vmem],
+        out_specs=(vmem, vmem),
+        scratch_shapes=[
+            pltpu.VMEM((2, zs, size, width), BF16),
+            pltpu.VMEM((2, far, size, width), BF16),
+            pltpu.VMEM((2, far, size, width), BF16),
+            pltpu.VMEM((2, far, rows, width), BF16),
+            pltpu.VMEM((2, far, rows, width), BF16),
+            pltpu.VMEM((x_count - 1, rows, width), BF16),
+            pltpu.VMEM((size, width), BF16),
+            pltpu.VMEM((zs, x_count - 1, rows, width), BF16),
+            pltpu.VMEM((zs, size, width), BF16),
+            pltpu.VMEM((2, zs, size, width), F32),
+        ]
+        + [dma(dims) for dims in sems],
+        compiler_params=pltpu.CompilerParams(
+            collective_id=1, has_side_effects=True, vmem_limit_bytes=32 * 1024 * 1024
+        ),
+    )(parts)
+
+
+def shards(q_rows, k_rows, v_rows, dout, positions):
+    queries, kv = gather(CHIPS_X, q_rows, k_rows, v_rows)
     own = lax.axis_index("inner") * lax.axis_size("outer") + lax.axis_index("outer")
     pb = positions[:: 2 * RUN] // RUN
-    attn_out, grad_q, dkv = attention(own.reshape(1), pb, mine[:, :q_width], dout, kv)
-    dkv = lax.psum_scatter(dkv, ("inner", "outer"), scatter_dimension=0, tiled=True)
-    return attn_out, grad_q, dkv[:, :kv_width], dkv[:, kv_width:]
+    attn_out, grad_q, dkv = attention(own.reshape(1), pb, queries, dout, kv.reshape(-1, 2 * DH))
+    grad_k, grad_v = scatter(CHIPS_X, dkv.reshape(kv.shape))
+    return attn_out, grad_q, grad_k, grad_v
 
 
 def solution(mesh):

time: 579 us -> 105 us (0.18)
  the two profiles are of different devices: /device:TPU:88 before, /device:TPU:1 now
where the time goes in v3:
time: 105 us; the launch traced here: 104 us
  Pallas kernels  98 us (93%)
  local copies, waits for them, and re-layouts  4.32 us (4%)
    pallas_call x1, Pallas kernels, gather(): pl.pallas_call(functools.partial(gather_kernel, x_count), out_shape=(jax....  49.6 us
    pallas_call x1, Pallas kernels, attention(): pl.pallas_call(attention_kernel, out_shape=(jax.ShapeDtypeStruct((rows, w...  24.3 us
    pallas_call x1, Pallas kernels, scatter(): pl.pallas_call(functools.partial(scatter_kernel, x_count), out_shape=(jax...  24.2 us
    unnamed x4, local copies, waits for them, and re-layouts  3.42 us

profile of v3, /device:TPU:1, one launch (start us, length us, event | category | flops | bytes accessed | tf_op | source)
XLA Modules:
  0.0 103.5 jit_solution(3628792287758665798)
XLA Ops:
  0.6 0.9 slice.3
  1.5 0.5 and_select_fusion.pb_ref
  2.1 49.6 %shard_map.84 = (bf16[128,512]{1,0:T(8,128)(2,1)}, bf16[2,16,256,256]{3,2,1,0:T(8,128)(2,1)}) custom-call(bf16[16,4096]{1,0:T(8,128)(2,1)} %q_ref.1, bf16[16,1024]{1,0:T(8,128)(2,1)} %k_ref.1, bf16[16,1024]{1,0:T(8,128)(2,1)} %v_ref.1), custom_call_target="tpu_custom_call" | custom-call | tf_op jit(solution)/shard_map/pallas_call | solution.py:440
  51.6 24.3 %shard_map.85 = (bf16[128,512]{1,0:T(8,128)(2,1)}, bf16[128,512]{1,0:T(8,128)(2,1)}, bf16[8192,256]{1,0:T(8,128)(2,1)}) custom-call(s32[1]{0:T(128)} %bitcast.own_ref, s32[64]{0:T(128)} %and_select_fusion.pb_ref, bf16[128,512]{1,0:T(8,128)(2,1)} %get-tuple-element.11.q_ref, bf16[128,512]{1,0:T(8,128)(2,1)} %do_ref.1, bf16[8192,256]{1,0:T(8,128)(2,1)} %bitcast.4), custom_call_target="tpu_custom_call" | custom-call | tf_op jit(solution)/shard_map/pallas_call | solution.py:175
  75.9 0.0 copy-start
  75.9 2.2 %copy-done = bf16[8192,256]{1,0:T(8,128)(2,1)S(1)} copy-done((bf16[8192,256]{1,0:T(8,128)(2,1)S(1)}, bf16[8192,256]{1,0:T(8,128)(2,1)}, u32[]{:S(2)}) %copy-start) | copy-done | bytes 4194328
  78.1 24.2 %shard_map.86 = (bf16[128,128]{1,0:T(8,128)(2,1)S(1)}, bf16[128,128]{1,0:T(8,128)(2,1)S(1)}) custom-call(bf16[2,16,256,256]{3,2,1,0:T(8,128)(2,1)S(1)} %bitcast.3), custom_call_target="tpu_custom_call" | custom-call | tf_op jit(solution)/shard_map/pallas_call | solution.py:635
  102.3 0.6 copy.11
  102.9 0.6 copy.12
Async XLA Ops:
  75.9 2.2 %copy-start = (bf16[8192,256]{1,0:T(8,128)(2,1)S(1)}, bf16[8192,256]{1,0:T(8,128)(2,1)}, u32[]{:S(2)}) copy-start(bf16[8192,256]{1,0:T(8,128)(2,1)} %get-tuple-element.15) | copy-start | bytes 12582916

commit v4 on v1

v4 whole, which is shorter than its diff:
```python
import functools

import jax
import jax.numpy as jnp
from jax import lax
from jax.experimental import pallas as pl
from jax.experimental.pallas import tpu as pltpu
from jax.sharding import PartitionSpec as P

QH = 32
KVH = 8
DH = 128
RUN = 64
BLOCKS = 64
CHIPS_X = 4
RATIO = QH // KVH
ROWS = RATIO * RUN
CHUNK = 256
RUNS_CHUNK = CHUNK // RUN
CHUNKS = 2 * BLOCKS // RUNS_CHUNK
ITEMS = CHUNKS + 1
LOG2E = 1.4426950408889634
SCALE = DH**-0.5
NEG_FILL = -1e30
F32 = jnp.float32
BF16 = jnp.bfloat16


def dot(a, b, ca, cb):
    return lax.dot_general(a, b, (((ca,), (cb,)), ((), ())), preferred_element_type=F32)


MESH = pl.DeviceIdType.MESH


class Plane:
    def __init__(self, x_count):
        inner, outer = lax.axis_index("inner"), lax.axis_index("outer")
        self.xs = x_count
        self.z_pairs = lax.axis_size("outer") // x_count
        self.zs = 2 * self.z_pairs
        self.x = lax.rem(outer, x_count)
        self.core = lax.rem(inner, 2)
        self.z = 2 * lax.div(outer, x_count) + lax.div(inner, 2)

    def z_off(self, by):
        return lax.rem(self.z + by + self.zs, self.zs)

    def x_off(self, by):
        return lax.rem(self.x + by + self.xs, self.xs)

    def group(self, z, core):
        return (2 * lax.rem(z, 2) + core) * self.z_pairs + lax.div(z, 2)

    def device(self, z=None, core=None, x=None):
        z = self.z if z is None else z
        core = self.core if core is None else core
        x = self.x if x is None else x
        return {"inner": 2 * lax.rem(z, 2) + core, "outer": lax.div(z, 2) * self.xs + x}

    def partners(self):
        found = [self.device(core=1 - self.core)]
        found += [self.device(z=self.z_off(1)), self.device(z=self.z_off(-1))]
        found += [self.device(x=self.x_off(d)) for d in range(1, self.xs)]
        return found

    def greet(self, heads=1):
        head = lax.axis_index("head")
        partners = [{"head": lax.rem(head + d, heads)} for d in range(1, heads)]
        partners += self.partners()
        barrier = pltpu.get_barrier_semaphore()
        for device in partners:
            pl.semaphore_signal(barrier, inc=1, device_id=device, device_id_type=MESH)
        pl.semaphore_wait(barrier, len(partners))


def push(src, dst, send_sem, recv_sem, device):
    copy = pltpu.make_async_remote_copy(
        src_ref=src,
        dst_ref=dst,
        send_sem=send_sem,
        recv_sem=recv_sem,
        device_id=device,
        device_id_type=MESH,
    )
    copy.start()
    return copy


def layer_kernel(
    x_count,
    pb_ref,
    q_ref,
    k_ref,
    v_ref,
    do_ref,
    out_ref,
    dq_ref,
    gk_ref,
    gv_ref,
    q_got,
    block,
    kv,
    qs,
    dos,
    s_full,
    s_mix,
    e_full,
    e_mix,
    e_own,
    top,
    peak,
    total,
    marks,
    acc_out,
    acc_dq,
    qd,
    dod,
    delta,
    parts,
    other,
    za_in,
    za_out,
    zb_in,
    zb_out,
    xa_in,
    xa_out,
    xb_in,
    xb_out,
    keep,
    y_send,
    y_recv,
    *sems,
):
    at = Plane(x_count)
    heads = lax.axis_size("head")
    far = at.zs // 2
    tokens = q_ref.shape[0]
    width = q_ref.shape[1] // heads
    rows = block.shape[0] // 2
    size = x_count * rows
    ga, gb, sa, sb = (sems[6 * i : 6 * i + 6] for i in range(4))
    at.greet(heads)

    head = lax.axis_index("head")
    here = pl.ds(pl.multiple_of(head * tokens, tokens), tokens)
    q_moves, kv_moves = [], []
    for d in range(1, heads):
        peer = lax.rem(head + d, heads)
        cols = pl.ds(pl.multiple_of(peer * DH, DH), DH)
        for i, src in enumerate((k_ref, v_ref)):
            kv_moves.append(
                push(
                    src.at[:, cols],
                    block.at[here, pl.ds(i * DH, DH)],
                    y_send.at[i, d - 1],
                    y_recv.at[i, d - 1],
                    {"head": peer},
                )
            )
    for d in range(1, heads):
        peer = lax.rem(head + d, heads)
        cols = pl.ds(pl.multiple_of(peer * width, width), width)
        q_moves.append(
            push(
                q_ref.at[:, cols],
                q_got.at[here, :],
                y_send.at[2, d - 1],
                y_recv.at[2, d - 1],
                {"head": peer},
            )
        )
    cols = pl.ds(pl.multiple_of(head * DH, DH), DH)
    block[here, :DH] = k_ref[:, cols]
    block[here, DH:] = v_ref[:, cols]
    q_got[here, :] = q_ref[:, pl.ds(pl.multiple_of(head * width, width), width)]
    for copy in kv_moves:
        copy.wait_recv()
    sent = kv_moves + q_moves

    mine = pl.ds(pl.multiple_of(at.x * rows, rows), rows)
    own = at.group(at.z, at.core)
    kv[0, own, mine, :] = block[:rows, :]
    kv[1, own, mine, :] = block[rows:, :]

    def towards(way):
        return at.device(z=at.z_off(1 - 2 * way))

    def beside(src, dst, send, recv):
        copies = [
            push(src, dst, send.at[d - 1], recv.at[d - 1], at.device(x=at.x_off(d)))
            for d in range(1, at.xs)
        ]
        sent.extend(copies)
        return copies

    def arrive(copies):
        for copy in copies:
            copy.wait_recv()

    def move_a(way, step, group):
        part = kv.at[0, group]
        if step == far - 1:
            part = kv.at[0, group, pl.ds(way * (size // 2), size // 2), :]
        copy = push(part, part, ga[2].at[way, step], ga[3].at[way, step], towards(way))
        sent.append(copy)
        return copy

    def move_b(way, step, group):
        place = mine
        if step == far - 1:
            place = pl.ds(pl.multiple_of(at.x * rows + way * (rows // 2), rows // 2), rows // 2)
        part = kv.at[1, group, place, :]
        copy = push(part, part, gb[2].at[way, step], gb[3].at[way, step], towards(way))
        sent.append(copy)
        return copy

    crosses = {}

    def cross(half, i, group):
        whole = kv.at[half, group]
        send, recv = (gb, ga)[1 - half][4:]
        copy = push(whole, whole, send.at[i], recv.at[i], at.device(core=1 - at.core))
        sent.append(copy)
        crosses[half, i] = copy

    def spread(i, group):
        part = kv.at[1, group, mine, :]
        return i, group, beside(part, part, gb[0].at[i], gb[1].at[i])

    def finish(spreads):
        for i, group, copies in spreads:
            arrive(copies)
            cross(1, i, group)

    def fold(x, op):
        return op(x.reshape(x.shape[0] // 8, 8, ROWS), axis=0)

    def gap(group, r):
        return pb_ref[x_count * own + at.x] - pb_ref[x_count * group + r]

    def early(group, r):
        return jnp.full((RUN, ROWS), gap(group, r), jnp.int32) >= 0

    def run(r):
        return slice(r * RUN, (r + 1) * RUN)

    def products(group, half, rows_ref):
        first, second = kv[0, group], kv[1, group]
        cols = slice(half * DH, (half + 1) * DH)
        return (
            dot(first[:, cols], rows_ref[1], 1, 1),
            dot(first[:, cols], rows_ref[0], 1, 1),
            dot(second[:, cols], rows_ref[1], 1, 1),
        )

    def score(slot, group):
        full, one, two = products(group, 0, qs)
        s_full[slot] = full
        tops = [top[0], jnp.maximum(top[1], fold(full, jnp.max))]
        for r in range(x_count):
            is_early = early(group, r)
            mix = jnp.where(is_early, one[run(r)], two[run(r)])
            s_mix[slot, run(r), :] = mix
            highest = fold(mix, jnp.max)
            tops[0] = jnp.maximum(tops[0], jnp.where(is_early[:8], highest, NEG_FILL))
            tops[1] = jnp.maximum(tops[1], jnp.where(is_early[:8], NEG_FILL, highest))
        top[0], top[1] = tops

    def score_own():
        full, one, two = products(own, 0, qs)
        s_full[0] = full
        key = lax.broadcasted_iota(jnp.int32, (RUN, ROWS), 0)
        row = lax.rem(lax.broadcasted_iota(jnp.int32, (RUN, ROWS), 1), RUN)
        tops = [top[0], jnp.maximum(top[1], fold(full, jnp.max))]
        for r in range(x_count):
            away = gap(own, r) * RUN
            for s, (tile, sign) in enumerate(((one, 1), (two, -1))):
                masked = jnp.where(key - row <= sign * away, tile[run(r)], NEG_FILL)
                s_mix[s, run(r), :] = masked
                tops[s] = jnp.maximum(tops[s], fold(masked, jnp.max))
        top[0], top[1] = tops

    def renew(batch):
        for s in range(2):
            highest = jnp.max(top[s], axis=0, keepdims=True)
            factor = jnp.exp2((peak[s, 0:1, :] - highest) * (SCALE * LOG2E))
            total[s] = total[s] * factor
            acc_out[s] = acc_out[s] * factor
            peak[s] = jnp.broadcast_to(highest, (8, ROWS))
            marks[batch, s] = jnp.broadcast_to(highest, (8, ROWS))

    def weigh(slot, group):
        highs = [peak[s, 0:1, :] * (SCALE * LOG2E) for s in range(2)]
        full = jnp.exp2(s_full[slot] * (SCALE * LOG2E) - highs[1])
        totals = [total[0], total[1] + fold(full, jnp.sum)]
        full = full.astype(BF16)
        e_full[group] = full
        ones, twos = [], []
        for r in range(x_count):
            is_early = early(group, r)
            high = jnp.where(is_early[:8], highs[0], highs[1])[0:1]
            e = jnp.exp2(s_mix[slot, run(r), :] * (SCALE * LOG2E) - high)
            e_mix[group, run(r), :] = e.astype(BF16)
            ones.append(jnp.where(is_early, e, 0.0))
            twos.append(jnp.where(is_early, 0.0, e))
            totals[0] = totals[0] + fold(ones[-1], jnp.sum)
            totals[1] = totals[1] + fold(twos[-1], jnp.sum)
        total[0], total[1] = totals
        add_out(group, full, ones, twos)

    def weigh_own():
        full = jnp.exp2((s_full[0] - peak[1, 0:1, :]) * (SCALE * LOG2E))
        one = jnp.exp2((s_mix[0] - peak[0, 0:1, :]) * (SCALE * LOG2E))
        two = jnp.exp2((s_mix[1] - peak[1, 0:1, :]) * (SCALE * LOG2E))
        total[0] = total[0] + fold(one, jnp.sum)
        total[1] = total[1] + fold(full, jnp.sum) + fold(two, jnp.sum)
        full = full.astype(BF16)
        e_full[own] = full
        e_own[0] = one.astype(BF16)
        e_own[1] = two.astype(BF16)
        add_out(own, full, [one], [two])

    def add_out(group, full, ones, twos):
        one = jnp.concatenate([e.astype(BF16) for e in ones], axis=0)
        two = jnp.concatenate([e.astype(BF16) for e in twos], axis=0)
        first = kv[0, group, :, DH:].T
        second = kv[1, group, :, DH:].T
        acc_out[0] = acc_out[0] + dot(first, one, 1, 0)
        acc_out[1] = acc_out[1] + dot(first, full, 1, 0) + dot(second, two, 1, 0)

    def forward(batch, count, group_of):
        def first(j, carry):
            score(j, group_of(j))
            return carry

        def then(j, carry):
            weigh(j, group_of(j))
            return carry

        lax.fori_loop(0, count, first, 0)
        renew(batch)
        lax.fori_loop(0, count, then, 0)

    a_first = beside(kv.at[0, own, mine, :], kv.at[0, own, mine, :], ga[0], ga[1])
    b_moves = [move_b(way, 0, own) for way in range(2)]
    spreads = [spread(0, own)]
    arrive(a_first)
    a_moves = [move_a(way, 0, own) for way in range(2)]
    cross(0, 0, own)
    arrive(q_moves)
    for s in range(2):
        for h in range(RATIO):
            cols = slice(h * DH, (h + 1) * DH)
            qs[s, run(h), :] = q_got[run(s), cols]
            dos[s, run(h), :] = do_ref[run(s), cols]
    top[...] = jnp.full(top.shape, NEG_FILL, F32)
    peak[...] = jnp.full(peak.shape, NEG_FILL, F32)
    total[...] = jnp.zeros(total.shape, F32)
    acc_out[...] = jnp.zeros(acc_out.shape, F32)
    acc_dq[...] = jnp.zeros(acc_dq.shape, F32)
    finish(spreads)
    score_own()
    renew(0)
    weigh_own()

    def both(by):
        return lambda j: at.group(
            at.z_off(by * (2 * lax.rem(j, 2) - 1)), lax.rem(at.core + lax.div(j, 2), 2)
        )

    def crossed(indices):
        for i in indices:
            for half in range(2):
                crosses[half, i].wait_recv()

    for step in range(far):
        groups = [at.group(at.z_off((2 * way - 1) * (step + 1)), at.core) for way in range(2)]
        last = step == far - 1
        spreads = []
        arrive(b_moves)
        if last:
            spreads.append(spread(2 * far - 1, groups[0]))
        else:
            b_moves = [move_b(way, step + 1, groups[way]) for way in range(2)]
            spreads = [spread(2 * step + 1 + way, groups[way]) for way in range(2)]
        if last:
            arrive(a_moves)
            cross(0, 2 * far - 1, groups[0])
        else:
            for way in range(2):
                a_moves[way].wait_recv()
                a_moves[way] = move_a(way, step + 1, groups[way])
                cross(0, 2 * step + 1 + way, groups[way])
        if step == 0:
            crossed([0])
            forward(1, 1, lambda j: at.group(at.z, 1 - at.core))
        else:
            crossed([2 * step - 1, 2 * step])
            forward(1 + step, 4, both(step))
        finish(spreads)
    crossed([2 * far - 1])
    forward(1 + far, 2, lambda j: at.group(at.z_off(far), lax.rem(at.core + j, 2)))

    for s in range(2):
        inv = 1.0 / jnp.sum(total[s], axis=0, keepdims=True)
        out = (acc_out[s] * inv).astype(BF16).astype(F32)
        d_rows = dos[s].astype(F32)
        q_part = qs[s].astype(F32) * SCALE
        delta[s] = jnp.broadcast_to(jnp.sum(out * d_rows.T, axis=0, keepdims=True), (8, ROWS))
        total[s] = jnp.broadcast_to(inv, (8, ROWS))
        for batch in range(far + 2):
            factor = jnp.exp2((marks[batch, s] - peak[s]) * (SCALE * LOG2E))
            marks[batch, s] = factor
            by_row = jnp.broadcast_to(factor[0:1] * inv, (DH, ROWS)).T
            dod[batch, s] = (d_rows * by_row).astype(BF16)
            qd[batch, s] = (q_part * by_row).astype(BF16)
        out = out.T.astype(BF16)
        for h in range(RATIO):
            out_ref[run(s), h * DH : (h + 1) * DH] = out[run(h)]

    def backward(group, batch, who, i, is_own=False):
        pf, p1, p2 = products(group, 1, dos)
        full = e_full[group]
        d_one, d_two = delta[0, 0:1, :], delta[1, 0:1, :]
        ds_full = (full.astype(F32) * (pf - d_two)).astype(BF16)
        if is_own:
            one, two = e_own[0], e_own[1]
            ds_one = (one.astype(F32) * (p1 - d_one)).astype(BF16)
            ds_two = (two.astype(F32) * (p2 - d_two)).astype(BF16)
        else:
            lists = [[], [], [], []]
            for r in range(x_count):
                is_early = early(group, r)
                e = e_mix[group, run(r), :].astype(F32)
                ds = e * jnp.where(is_early, p1[run(r)] - d_one, p2[run(r)] - d_two)
                for x, (to_one, to_two) in ((e, lists[:2]), (ds, lists[2:])):
                    to_one.append(jnp.where(is_early, x, 0.0).astype(BF16))
                    to_two.append(jnp.where(is_early, 0.0, x).astype(BF16))
            one, two, ds_one, ds_two = (jnp.concatenate(x, axis=0) for x in lists)
        parts[who, 0, i, :, :DH] = (
            dot(ds_full, qd[batch, 1], 1, 0) + dot(ds_one, qd[batch, 0], 1, 0)
        ).astype(BF16)
        parts[who, 0, i, :, DH:] = (
            dot(full, dod[batch, 1], 1, 0) + dot(one, dod[batch, 0], 1, 0)
        ).astype(BF16)
        parts[who, 1, i, :, :DH] = dot(ds_two, qd[batch, 1], 1, 0).astype(BF16)
        parts[who, 1, i, :, DH:] = dot(two, dod[batch, 1], 1, 0).astype(BF16)
        first = kv[0, group, :, :DH].T
        second = kv[1, group, :, :DH].T
        acc_dq[0] = acc_dq[0] + marks[batch, 0, 0:1, :] * dot(first, ds_one, 1, 0)
        acc_dq[1] = acc_dq[1] + marks[batch, 1, 0:1, :] * (
            dot(first, ds_full, 1, 0) + dot(second, ds_two, 1, 0)
        )

    hand_over = {}

    def give(i):
        for half in (1, 0):
            send, recv = (sb, sa)[1 - half][4:]
            copy = push(
                parts.at[0, half, i],
                other.at[half, i],
                send.at[i],
                recv.at[i],
                at.device(core=1 - at.core),
            )
            sent.append(copy)
            hand_over[half, i] = copy

    def pair(half, i):
        hand_over[half, i].wait_recv()
        return parts[1, half, i].astype(F32) + other[half, i].astype(F32)

    def across(src, dst, send, recv):
        copies = []
        for d in range(1, at.xs):
            x = at.x_off(d)
            place = pl.ds(pl.multiple_of(x * rows, rows), rows)
            copies.append(
                push(src.at[place, :], dst.at[d - 1], send.at[d - 1], recv.at[d - 1], at.device(x=x))
            )
        sent.extend(copies)
        return copies

    def spread_b(i):
        both_cores = pair(1, i)
        keep[i] = both_cores
        xb_out[i] = both_cores.astype(BF16)
        return across(xb_out.at[i], xb_in.at[i], sb[0].at[i], sb[1].at[i])

    def collect(copies, kept, arrived):
        summed = kept[mine, :]
        for d in range(1, at.xs):
            copies[d - 1].wait_recv()
            summed = summed + arrived[d - 1].astype(F32)
        return summed

    def collect_b(i):
        return collect(b_spreads[i], keep.at[i], xb_in.at[i])

    def half_of(way, length):
        return slice(way * (length // 2), (way + 1) * (length // 2))

    def along(out, into, sems, way, step):
        length = out.shape[2]
        place = pl.ds(way * (length // 2), length // 2) if step == 0 else pl.ds(0, length)
        copy = push(
            out.at[way, step, place, :],
            into.at[way, step, place, :],
            sems[2].at[way, step],
            sems[3].at[way, step],
            towards(way),
        )
        sent.append(copy)
        return copy

    def begin(summed, out, into, sems):
        moves = []
        for way in range(2):
            place = half_of(way, out.shape[2])
            out[way, 0, place, :] = summed[place].astype(BF16)
            moves.append(along(out, into, sems, way, 0))
        return moves

    def go_on(moves, way, step, summed, out, into, sems):
        moves[way].wait_recv()
        if step == 1:
            near, rest = half_of(way, out.shape[2]), half_of(1 - way, out.shape[2])
            out[way, 1, near, :] = (summed[near] + into[way, 0, near, :].astype(F32)).astype(BF16)
            out[way, 1, rest, :] = summed[rest].astype(BF16)
        else:
            out[way, step] = (summed + into[way, step - 1].astype(F32)).astype(BF16)
        moves[way] = along(out, into, sems, way, step)

    def end(moves, summed, into):
        for way in range(2):
            moves[way].wait_recv()
            summed = summed + into[way, far - 1].astype(F32)
        return summed

    def back(who, step):
        core = lax.rem(at.core + 1 + who, 2)

        def one_way(way, carry):
            offset = (far - step) * (1 - 2 * way)
            group = at.group(at.z_off(offset), core)
            backward(group, 1 + far - step, who, 2 * step - 1 + way)
            return carry

        lax.fori_loop(0, 2, one_way, 0)

    a_refs = (za_out, za_in, sa)
    b_refs = (zb_out, zb_in, sb)
    backward(at.group(at.z_off(far), 1 - at.core), 1 + far, 0, 0)
    give(0)
    backward(at.group(at.z_off(far), at.core), 1 + far, 1, 0)
    b_spreads = {0: spread_b(0)}
    a_moves = begin(pair(0, 0), *a_refs)
    b_moves = None
    for step in range(1, far):
        back(0, step)
        give(2 * step - 1)
        give(2 * step)
        back(1, step)
        for way in range(2):
            b_spreads[2 * step - 1 + way] = spread_b(2 * step - 1 + way)
        for way in range(2):
            go_on(a_moves, way, step, pair(0, 2 * step - 1 + way), *a_refs)
        if step == 1:
            b_moves = begin(collect_b(0), *b_refs)
        else:
            for way in range(2):
                go_on(b_moves, way, step - 1, collect_b(2 * step - 3 + way), *b_refs)
    backward(at.group(at.z, 1 - at.core), 1, 0, at.zs - 1)
    give(at.zs - 1)
    for way in range(2):
        go_on(b_moves, way, far - 1, collect_b(2 * far - 3 + way), *b_refs)
    backward(own, 0, 1, at.zs - 1, True)
    b_spreads[at.zs - 1] = spread_b(at.zs - 1)
    mine_a = end(a_moves, pair(0, at.zs - 1), za_in)
    other_a = keep.at[0]
    other_a[...] = mine_a
    xa_out[...] = mine_a.astype(BF16)
    last_a = across(xa_out, xa_in, sa[0], sa[1])
    for s in range(2):
        grad = (acc_dq[s] * (total[s, 0:1, :] * SCALE)).T.astype(BF16)
        for h in range(RATIO):
            dq_ref[run(s), h * DH : (h + 1) * DH] = grad[run(h)]
    second = end(b_moves, collect_b(at.zs - 1), zb_in)
    gk_ref[rows:, :] = second[:, :DH].astype(BF16)
    gv_ref[rows:, :] = second[:, DH:].astype(BF16)
    first = collect(last_a, keep.at[0], xa_in)
    gk_ref[:rows, :] = first[:, :DH].astype(BF16)
    gv_ref[:rows, :] = first[:, DH:].astype(BF16)
    for copy in sent:
        copy.wait_send()


def layer(x_count, pb, q_rows, k_rows, v_rows, dout):
    heads = lax.axis_size("head")
    rows = heads * q_rows.shape[0]
    width = q_rows.shape[1] // heads
    zs = 2 * (lax.axis_size("outer") // x_count)
    far = zs // 2
    run = rows // 2
    size = x_count * run
    batches = far + 2
    kv_width = 2 * DH
    dma = pltpu.SemaphoreType.DMA
    vmem = pl.BlockSpec(memory_space=pltpu.VMEM)
    sems = [(3, heads - 1), (3, heads - 1)]
    for x_dims in ((x_count - 1,), (zs, x_count - 1)) * 2:
        sems += [x_dims, x_dims, (2, far), (2, far), (zs,), (zs,)]
    buffers = [
        ((rows, width), BF16),
        ((rows, kv_width), BF16),
        ((2, 2 * zs, size, kv_width), BF16),
        ((2, ROWS, DH), BF16),
        ((2, ROWS, DH), BF16),
        ((4, size, ROWS), F32),
        ((4, size, ROWS), F32),
        ((2 * zs, size, ROWS), BF16),
        ((2 * zs, size, ROWS), BF16),
        ((2, size, ROWS), BF16),
        ((2, 8, ROWS), F32),
        ((2, 8, ROWS), F32),
        ((2, 8, ROWS), F32),
        ((batches, 2, 8, ROWS), F32),
        ((2, DH, ROWS), F32),
        ((2, DH, ROWS), F32),
        ((batches, 2, ROWS, DH), BF16),
        ((batches, 2, ROWS, DH), BF16),
        ((2, 8, ROWS), F32),
        ((2, 2, zs, size, kv_width), BF16),
        ((2, zs, size, kv_width), BF16),
        ((2, far, size, kv_width), BF16),
        ((2, far, size, kv_width), BF16),
        ((2, far, run, kv_width), BF16),
        ((2, far, run, kv_width), BF16),
        ((x_count - 1, run, kv_width), BF16),
        ((size, kv_width), BF16),
        ((zs, x_count - 1, run, kv_width), BF16),
        ((zs, size, kv_width), BF16),
        ((zs, size, kv_width), F32),
    ]
    return pl.pallas_call(
        functools.partial(layer_kernel, x_count),
        out_shape=(jax.ShapeDtypeStruct((rows, width), BF16),) * 2
        + (jax.ShapeDtypeStruct((rows, DH), BF16),) * 2,
        in_specs=[pl.BlockSpec(memory_space=pltpu.SMEM)] + [vmem] * 4,
        out_specs=(vmem,) * 4,
        scratch_shapes=[pltpu.VMEM(dims, kind) for dims, kind in buffers]
        + [dma(dims) for dims in sems],
        compiler_params=pltpu.CompilerParams(
            collective_id=0, has_side_effects=True, vmem_limit_bytes=56 * 1024 * 1024
        ),
    )(pb, q_rows, k_rows, v_rows, dout)


def shards(q_rows, k_rows, v_rows, dout, positions):
    return layer(CHIPS_X, positions[:: 2 * RUN] // RUN, q_rows, k_rows, v_rows, dout)


def solution(mesh):
    return jax.shard_map(
        shards,
        mesh=mesh,
        in_specs=(
            P(("inner", "outer", "head"), None),
            P(("inner", "outer", "head"), None),
            P(("inner", "outer", "head"), None),
            P(("inner", "outer"), "head"),
            P(),
        ),
        out_specs=(
            P(("inner", "outer"), "head"),
            P(("inner", "outer"), "head"),
            P(("inner", "outer"), "head"),
            P(("inner", "outer"), "head"),
        ),
        check_vma=False,
    )
```

time: 579 us -> 83.6 us (0.14)
  the two profiles are of different devices: /device:TPU:88 before, /device:TPU:1 now
where the time goes in v4:
time: 83.6 us; the launch traced here: 83.3 us
  Pallas kernels  77.4 us (93%)
  local copies, waits for them, and re-layouts  4.65 us (6%)
    pallas_call x1, Pallas kernels, layer(): pl.pallas_call(functools.partial(layer_kernel, x_count), out_shape=(jax.S...  77.4 us
    unnamed x10, local copies, waits for them, and re-layouts  3.75 us

profile of v4, /device:TPU:1, one launch (start us, length us, event | category | flops | bytes accessed | tf_op | source)
XLA Modules:
  0.0 83.3 jit_solution(3977049061474829226)
XLA Ops:
  0.6 0.9 %slice.3 = s32[64]{0:T(128)S(1)} slice(s32[8192]{0:T(1024)} %param.9), slice={[0:8192:128]} | slice | bytes 512 | tf_op jit(solution)/shard_map/slice | solution.py:662
  1.5 0.5 and_select_fusion.pb_ref
  2.1 77.4 %shard_map.84 = (bf16[128,512]{1,0:T(8,128)(2,1)}, bf16[128,512]{1,0:T(8,128)(2,1)}, bf16[128,128]{1,0:T(8,128)(2,1)}, bf16[128,128]{1,0:T(8,128)(2,1)}) custom-call(s32[64]{0:T(128)} %and_select_fusion.pb_ref, bf16[16,4096]{1,0:T(8,128)(2,1)} %q_ref.1, bf16[16,1024]{1,0:T(8,128)(2,1)} %k_ref.1, bf16[16,1024]{1,0:T(8,128)(2,1)} %v_ref.1, bf16[128,512]{1,0:T(8,128)(2,1)} %do_ref.1), custom_call_target="tpu_custom_call" | custom-call | tf_op jit(solution)/shard_map/pallas_call | solution.py:647
  79.5 0.0 copy-start
  79.5 1.6 %copy.13 = bf16[128,512]{1,0:T(8,128)(2,1)} copy(bf16[128,512]{1,0:T(8,128)(2,1)} %get-tuple-element.8) | data formatting | bytes 262144
  81.1 0.0 copy-done
  81.1 0.0 copy-start.2
  81.1 0.7 copy.14
  81.8 0.1 copy-done.2
  81.9 0.0 copy-start.1
  81.9 0.6 copy.15
  82.5 0.2 copy-done.1
  82.6 0.6 copy.16
Async XLA Ops:
  79.5 1.6 %copy-start = (bf16[128,512]{1,0:T(8,128)(2,1)S(1)}, bf16[128,512]{1,0:T(8,128)(2,1)}, u32[]{:S(2)}) copy-start(bf16[128,512]{1,0:T(8,128)(2,1)} %get-tuple-element.9) | copy-start | bytes 393220
  81.1 0.8 copy-start.2
  81.9 0.8 copy-start.1

commit v5 on v4

--- a/solution.py
+++ b/solution.py
@@ -89,7 +89,7 @@
 
 def layer_kernel(
     x_count,
-    pb_ref,
+    pos_ref,
     q_ref,
     k_ref,
     v_ref,
@@ -108,6 +108,13 @@
     e_full,
     e_mix,
     e_own,
+    km,
+    vm,
+    km_t,
+    ka_t,
+    dp_full,
+    dp_mix,
+    vm_t,
     top,
     peak,
     total,
@@ -237,77 +244,89 @@
         return op(x.reshape(x.shape[0] // 8, 8, ROWS), axis=0)
 
     def gap(group, r):
-        return pb_ref[x_count * own + at.x] - pb_ref[x_count * group + r]
-
-    def early(group, r):
-        return jnp.full((RUN, ROWS), gap(group, r), jnp.int32) >= 0
+        mine_first = pos_ref[(x_count * own + at.x) * 2 * rows]
+        return mine_first - pos_ref[(x_count * group + r) * 2 * rows]
+
+    def early(group, r, shape=(RUN, ROWS)):
+        return jnp.full(shape, gap(group, r), jnp.int32) >= 0
 
     def run(r):
         return slice(r * RUN, (r + 1) * RUN)
 
-    def products(group, half, rows_ref):
+    def prepare(group):
         first, second = kv[0, group], kv[1, group]
-        cols = slice(half * DH, (half + 1) * DH)
-        return (
-            dot(first[:, cols], rows_ref[1], 1, 1),
-            dot(first[:, cols], rows_ref[0], 1, 1),
-            dot(second[:, cols], rows_ref[1], 1, 1),
-        )
+        for r in range(x_count):
+            is_early = early(group, r, (RUN, 2 * DH))
+            left = jnp.where(is_early, first[run(r)].astype(F32), 0.0).astype(BF16)
+            right = jnp.where(is_early, 0.0, second[run(r)].astype(F32)).astype(BF16)
+            km[group, run(r), :] = jnp.concatenate([left[:, :DH], right[:, :DH]], axis=1)
+            vm[run(r), :] = jnp.concatenate([left[:, DH:], right[:, DH:]], axis=1)
+        km_t[group] = km[group].T
+        ka_t[group] = first[:, :DH].T
+        dp_full[group] = dot(first[:, DH:], dos[:, DH:], 1, 1)
+        dp_mix[group] = dot(vm[...], dos[...], 1, 1)
+        return vm[...].T
 
     def score(slot, group):
-        full, one, two = products(group, 0, qs)
+        full = dot(kv[0, group, :, :DH], qs[:, DH:], 1, 1)
+        vm_t[slot] = prepare(group)
+        mix = dot(km[group], qs[...], 1, 1)
         s_full[slot] = full
+        s_mix[slot] = mix
         tops = [top[0], jnp.maximum(top[1], fold(full, jnp.max))]
         for r in range(x_count):
-            is_early = early(group, r)
-            mix = jnp.where(is_early, one[run(r)], two[run(r)])
-            s_mix[slot, run(r), :] = mix
-            highest = fold(mix, jnp.max)
-            tops[0] = jnp.maximum(tops[0], jnp.where(is_early[:8], highest, NEG_FILL))
-            tops[1] = jnp.maximum(tops[1], jnp.where(is_early[:8], NEG_FILL, highest))
+            is_early = early(group, r, (8, ROWS))
+            highest = fold(mix[run(r)], jnp.max)
+            tops[0] = jnp.maximum(tops[0], jnp.where(is_early, highest, NEG_FILL))
+            tops[1] = jnp.maximum(tops[1], jnp.where(is_early, NEG_FILL, highest))
         top[0], top[1] = tops
 
     def score_own():
-        full, one, two = products(own, 0, qs)
+        first, second = kv[0, own, :, :DH], kv[1, own, :, :DH]
+        full = dot(first, qs[:, DH:], 1, 1)
+        one = dot(first, qs[:, :DH], 1, 1)
+        two = dot(second, qs[:, DH:], 1, 1)
         s_full[0] = full
         key = lax.broadcasted_iota(jnp.int32, (RUN, ROWS), 0)
         row = lax.rem(lax.broadcasted_iota(jnp.int32, (RUN, ROWS), 1), RUN)
         tops = [top[0], jnp.maximum(top[1], fold(full, jnp.max))]
         for r in range(x_count):
-            away = gap(own, r) * RUN
+            away = gap(own, r)
             for s, (tile, sign) in enumerate(((one, 1), (two, -1))):
                 masked = jnp.where(key - row <= sign * away, tile[run(r)], NEG_FILL)
                 s_mix[s, run(r), :] = masked
                 tops[s] = jnp.maximum(tops[s], fold(masked, jnp.max))
         top[0], top[1] = tops
 
+    def part(s):
+        return slice(s * DH, (s + 1) * DH)
+
     def renew(batch):
         for s in range(2):
             highest = jnp.max(top[s], axis=0, keepdims=True)
             factor = jnp.exp2((peak[s, 0:1, :] - highest) * (SCALE * LOG2E))
             total[s] = total[s] * factor
-            acc_out[s] = acc_out[s] * factor
+            acc_out[part(s), :] = acc_out[part(s), :] * factor
             peak[s] = jnp.broadcast_to(highest, (8, ROWS))
             marks[batch, s] = jnp.broadcast_to(highest, (8, ROWS))
 
     def weigh(slot, group):
-        highs = [peak[s, 0:1, :] * (SCALE * LOG2E) for s in range(2)]
-        full = jnp.exp2(s_full[slot] * (SCALE * LOG2E) - highs[1])
+        highs = [peak[s] * (SCALE * LOG2E) for s in range(2)]
+        full = jnp.exp2(s_full[slot] * (SCALE * LOG2E) - highs[1][0:1])
         totals = [total[0], total[1] + fold(full, jnp.sum)]
         full = full.astype(BF16)
         e_full[group] = full
-        ones, twos = [], []
         for r in range(x_count):
-            is_early = early(group, r)
-            high = jnp.where(is_early[:8], highs[0], highs[1])[0:1]
+            is_early = early(group, r, (8, ROWS))
+            high = jnp.where(is_early, highs[0], highs[1])[0:1]
             e = jnp.exp2(s_mix[slot, run(r), :] * (SCALE * LOG2E) - high)
             e_mix[group, run(r), :] = e.astype(BF16)
-            ones.append(jnp.where(is_early, e, 0.0))
-            twos.append(jnp.where(is_early, 0.0, e))
-            totals[0] = totals[0] + fold(ones[-1], jnp.sum)
-            totals[1] = totals[1] + fold(twos[-1], jnp.sum)
+            summed = fold(e, jnp.sum)
+            totals[0] = totals[0] + jnp.where(is_early, summed, 0.0)
+            totals[1] = totals[1] + jnp.where(is_early, 0.0, summed)
         total[0], total[1] = totals
-        add_out(group, full, ones, twos)
+        acc_out[...] = acc_out[...] + dot(vm_t[slot], e_mix[group], 1, 0)
+        acc_out[DH:, :] = acc_out[DH:, :] + dot(kv[0, group, :, DH:].T, full, 1, 0)
 
     def weigh_own():
         full = jnp.exp2((s_full[0] - peak[1, 0:1, :]) * (SCALE * LOG2E))
@@ -315,19 +334,14 @@
         two = jnp.exp2((s_mix[1] - peak[1, 0:1, :]) * (SCALE * LOG2E))
         total[0] = total[0] + fold(one, jnp.sum)
         total[1] = total[1] + fold(full, jnp.sum) + fold(two, jnp.sum)
-        full = full.astype(BF16)
-        e_full[own] = full
+        e_full[own] = full.astype(BF16)
         e_own[0] = one.astype(BF16)
         e_own[1] = two.astype(BF16)
-        add_out(own, full, [one], [two])
-
-    def add_out(group, full, ones, twos):
-        one = jnp.concatenate([e.astype(BF16) for e in ones], axis=0)
-        two = jnp.concatenate([e.astype(BF16) for e in twos], axis=0)
-        first = kv[0, group, :, DH:].T
-        second = kv[1, group, :, DH:].T
-        acc_out[0] = acc_out[0] + dot(first, one, 1, 0)
-        acc_out[1] = acc_out[1] + dot(first, full, 1, 0) + dot(second, two, 1, 0)
+        first, second = kv[0, own, :, DH:].T, kv[1, own, :, DH:].T
+        acc_out[:DH, :] = acc_out[:DH, :] + dot(first, e_own[0], 1, 0)
+        acc_out[DH:, :] = (
+            acc_out[DH:, :] + dot(first, e_full[own], 1, 0) + dot(second, e_own[1], 1, 0)
+        )
 
     def forward(batch, count, group_of):
         def first(j, carry):
@@ -352,8 +366,8 @@
     for s in range(2):
         for h in range(RATIO):
             cols = slice(h * DH, (h + 1) * DH)
-            qs[s, run(h), :] = q_got[run(s), cols]
-            dos[s, run(h), :] = do_ref[run(s), cols]
+            qs[run(h), part(s)] = q_got[run(s), cols]
+            dos[run(h), part(s)] = do_ref[run(s), cols]
     top[...] = jnp.full(top.shape, NEG_FILL, F32)
     peak[...] = jnp.full(peak.shape, NEG_FILL, F32)
     total[...] = jnp.zeros(total.shape, F32)
@@ -404,52 +418,69 @@
 
     for s in range(2):
         inv = 1.0 / jnp.sum(total[s], axis=0, keepdims=True)
-        out = (acc_out[s] * inv).astype(BF16).astype(F32)
-        d_rows = dos[s].astype(F32)
-        q_part = qs[s].astype(F32) * SCALE
+        out = (acc_out[part(s), :] * inv).astype(BF16).astype(F32)
+        d_rows = dos[:, part(s)].astype(F32)
+        q_part = qs[:, part(s)].astype(F32) * SCALE
         delta[s] = jnp.broadcast_to(jnp.sum(out * d_rows.T, axis=0, keepdims=True), (8, ROWS))
         total[s] = jnp.broadcast_to(inv, (8, ROWS))
         for batch in range(far + 2):
             factor = jnp.exp2((marks[batch, s] - peak[s]) * (SCALE * LOG2E))
             marks[batch, s] = factor
             by_row = jnp.broadcast_to(factor[0:1] * inv, (DH, ROWS)).T
-            dod[batch, s] = (d_rows * by_row).astype(BF16)
-            qd[batch, s] = (q_part * by_row).astype(BF16)
+            dod[batch, :, part(s)] = (d_rows * by_row).astype(BF16)
+            qd[batch, :, part(s)] = (q_part * by_row).astype(BF16)
         out = out.T.astype(BF16)
         for h in range(RATIO):
             out_ref[run(s), h * DH : (h + 1) * DH] = out[run(h)]
 
-    def backward(group, batch, who, i, is_own=False):
-        pf, p1, p2 = products(group, 1, dos)
-        full = e_full[group]
+    def backward(group, batch, who, i):
+        full, mix = e_full[group], e_mix[group]
+        ds_full = (full.astype(F32) * (dp_full[group] - delta[1, 0:1, :])).astype(BF16)
+        ds_mix = []
+        for r in range(x_count):
+            shift = jnp.where(early(group, r, (8, ROWS)), delta[0], delta[1])[0:1]
+            e = e_mix[group, run(r), :].astype(F32)
+            ds_mix.append((e * (dp_mix[group, run(r), :] - shift)).astype(BF16))
+        ds_mix = jnp.concatenate(ds_mix, axis=0)
+        for cols, left, right, scaled in (
+            (slice(0, DH), ds_full, ds_mix, qd),
+            (slice(DH, 2 * DH), full, mix, dod),
+        ):
+            whole = dot(left, scaled[batch, :, DH:], 1, 0)
+            mixed = dot(right, scaled[batch], 1, 0)
+            for r in range(x_count):
+                is_early = early(group, r, (RUN, DH))
+                first = whole[run(r)] + jnp.where(is_early, mixed[run(r), :DH], 0.0)
+                second = jnp.where(is_early, 0.0, mixed[run(r), DH:])
+                parts[who, 0, i, run(r), cols] = first.astype(BF16)
+                parts[who, 1, i, run(r), cols] = second.astype(BF16)
+        grad = dot(km_t[group], ds_mix, 1, 0)
+        late = grad[DH:] + dot(ka_t[group], ds_full, 1, 0)
+        acc_dq[:DH, :] = acc_dq[:DH, :] + marks[batch, 0, 0:1, :] * grad[:DH]
+        acc_dq[DH:, :] = acc_dq[DH:, :] + marks[batch, 1, 0:1, :] * late
+
+    def backward_own(i):
+        first, second = kv[0, own], kv[1, own]
         d_one, d_two = delta[0, 0:1, :], delta[1, 0:1, :]
-        ds_full = (full.astype(F32) * (pf - d_two)).astype(BF16)
-        if is_own:
-            one, two = e_own[0], e_own[1]
-            ds_one = (one.astype(F32) * (p1 - d_one)).astype(BF16)
-            ds_two = (two.astype(F32) * (p2 - d_two)).astype(BF16)
-        else:
-            lists = [[], [], [], []]
-            for r in range(x_count):
-                is_early = early(group, r)
-                e = e_mix[group, run(r), :].astype(F32)
-                ds = e * jnp.where(is_early, p1[run(r)] - d_one, p2[run(r)] - d_two)
-                for x, (to_one, to_two) in ((e, lists[:2]), (ds, lists[2:])):
-                    to_one.append(jnp.where(is_early, x, 0.0).astype(BF16))
-                    to_two.append(jnp.where(is_early, 0.0, x).astype(BF16))
-            one, two, ds_one, ds_two = (jnp.concatenate(x, axis=0) for x in lists)
-        parts[who, 0, i, :, :DH] = (
-            dot(ds_full, qd[batch, 1], 1, 0) + dot(ds_one, qd[batch, 0], 1, 0)
-        ).astype(BF16)
-        parts[who, 0, i, :, DH:] = (
-            dot(full, dod[batch, 1], 1, 0) + dot(one, dod[batch, 0], 1, 0)
-        ).astype(BF16)
-        parts[who, 1, i, :, :DH] = dot(ds_two, qd[batch, 1], 1, 0).astype(BF16)
-        parts[who, 1, i, :, DH:] = dot(two, dod[batch, 1], 1, 0).astype(BF16)
-        first = kv[0, group, :, :DH].T
-        second = kv[1, group, :, :DH].T
-        acc_dq[0] = acc_dq[0] + marks[batch, 0, 0:1, :] * dot(first, ds_one, 1, 0)
-        acc_dq[1] = acc_dq[1] + marks[batch, 1, 0:1, :] * (
+
+        def ds(e, values, s, shift):
+            dp = dot(values[:, DH:], dos[:, part(s)], 1, 1)
+            return (e.astype(F32) * (dp - shift)).astype(BF16)
+
+        ds_full = ds(e_full[own], first, 1, d_two)
+        ds_one = ds(e_own[0], first, 0, d_one)
+        ds_two = ds(e_own[1], second, 1, d_two)
+        for cols, full, one, two, scaled in (
+            (slice(0, DH), ds_full, ds_one, ds_two, qd),
+            (slice(DH, 2 * DH), e_full[own], e_own[0], e_own[1], dod),
+        ):
+            parts[1, 0, i, :, cols] = (
+                dot(full, scaled[0, :, DH:], 1, 0) + dot(one, scaled[0, :, :DH], 1, 0)
+            ).astype(BF16)
+            parts[1, 1, i, :, cols] = dot(two, scaled[0, :, DH:], 1, 0).astype(BF16)
+        first, second = first[:, :DH].T, second[:, :DH].T
+        acc_dq[:DH, :] = acc_dq[:DH, :] + marks[0, 0, 0:1, :] * dot(first, ds_one, 1, 0)
+        acc_dq[DH:, :] = acc_dq[DH:, :] + marks[0, 1, 0:1, :] * (
             dot(first, ds_full, 1, 0) + dot(second, ds_two, 1, 0)
         )
 
@@ -576,7 +607,7 @@
     give(at.zs - 1)
     for way in range(2):
         go_on(b_moves, way, far - 1, collect_b(2 * far - 3 + way), *b_refs)
-    backward(own, 0, 1, at.zs - 1, True)
+    backward_own(at.zs - 1)
     b_spreads[at.zs - 1] = spread_b(at.zs - 1)
     mine_a = end(a_moves, pair(0, at.zs - 1), za_in)
     other_a = keep.at[0]
@@ -584,7 +615,7 @@
     xa_out[...] = mine_a.astype(BF16)
     last_a = across(xa_out, xa_in, sa[0], sa[1])
     for s in range(2):
-        grad = (acc_dq[s] * (total[s, 0:1, :] * SCALE)).T.astype(BF16)
+        grad = (acc_dq[part(s), :] * (total[s, 0:1, :] * SCALE)).T.astype(BF16)
         for h in range(RATIO):
             dq_ref[run(s), h * DH : (h + 1) * DH] = grad[run(h)]
     second = end(b_moves, collect_b(at.zs - 1), zb_in)
@@ -597,7 +628,7 @@
         copy.wait_send()
 
 
-def layer(x_count, pb, q_rows, k_rows, v_rows, dout):
+def layer(x_count, positions, q_rows, k_rows, v_rows, dout):
     heads = lax.axis_size("head")
     rows = heads * q_rows.shape[0]
     width = q_rows.shape[1] // heads
@@ -616,21 +647,28 @@
         ((rows, width), BF16),
         ((rows, kv_width), BF16),
         ((2, 2 * zs, size, kv_width), BF16),
-        ((2, ROWS, DH), BF16),
-        ((2, ROWS, DH), BF16),
+        ((ROWS, 2 * DH), BF16),
+        ((ROWS, 2 * DH), BF16),
         ((4, size, ROWS), F32),
         ((4, size, ROWS), F32),
         ((2 * zs, size, ROWS), BF16),
         ((2 * zs, size, ROWS), BF16),
         ((2, size, ROWS), BF16),
+        ((2 * zs, size, kv_width), BF16),
+        ((size, kv_width), BF16),
+        ((2 * zs, kv_width, size), BF16),
+        ((2 * zs, DH, size), BF16),
+        ((2 * zs, size, ROWS), F32),
+        ((2 * zs, size, ROWS), F32),
+        ((4, kv_width, size), BF16),
         ((2, 8, ROWS), F32),
         ((2, 8, ROWS), F32),
         ((2, 8, ROWS), F32),
         ((batches, 2, 8, ROWS), F32),
-        ((2, DH, ROWS), F32),
-        ((2, DH, ROWS), F32),
-        ((batches, 2, ROWS, DH), BF16),
-        ((batches, 2, ROWS, DH), BF16),
+        ((2 * DH, ROWS), F32),
+        ((2 * DH, ROWS), F32),
+        ((batches, ROWS, 2 * DH), BF16),
+        ((batches, ROWS, 2 * DH), BF16),
         ((2, 8, ROWS), F32),
         ((2, 2, zs, size, kv_width), BF16),
         ((2, zs, size, kv_width), BF16),
@@ -655,11 +693,27 @@
         compiler_params=pltpu.CompilerParams(
             collective_id=0, has_side_effects=True, vmem_limit_bytes=56 * 1024 * 1024
         ),
-    )(pb, q_rows, k_rows, v_rows, dout)
+    )(positions, q_rows, k_rows, v_rows, dout)
+
+
+def hand_in_kernel(*refs):
+    half = len(refs) // 2
+    for src, dst in zip(refs[:half], refs[half:]):
+        dst[...] = src[...]
+
+
+def hand_in(*results):
+    vmem = pl.BlockSpec(memory_space=pltpu.VMEM)
+    return pl.pallas_call(
+        hand_in_kernel,
+        out_shape=tuple(jax.ShapeDtypeStruct(x.shape, x.dtype) for x in results),
+        in_specs=[vmem] * len(results),
+        out_specs=(vmem,) * len(results),
+    )(*results)
 
 
 def shards(q_rows, k_rows, v_rows, dout, positions):
-    return layer(CHIPS_X, positions[:: 2 * RUN] // RUN, q_rows, k_rows, v_rows, dout)
+    return hand_in(*layer(CHIPS_X, positions, q_rows, k_rows, v_rows, dout))
 
 
 def solution(mesh):

time: 83.6 us -> 80.4 us (0.962)
  local copies, waits for them, and re-layouts: 4.65 us -> 0 us
  Pallas kernels: 77.4 us -> 79.5 us
    unnamed x10 -> x0, local copies, waits for them, and re-layouts: 3.75 us -> none
    pallas_call x0 -> x1, Pallas kernels: none -> 1.7 us  [hand_in(): pl.pallas_call(hand_in_kernel, out_shape=tuple((jax.ShapeDtypeStruct(x.sh...]
    slice x1 -> x0, local copies, waits for them, and re-layouts: 0.9 us -> none  [shards(): positions[::2 * RUN] // RUN]
where the time goes in v5:
time: 80.4 us; the launch traced here: 80.2 us
  Pallas kernels  79.5 us (99%)
    pallas_call x1, Pallas kernels, layer(): pl.pallas_call(functools.partial(layer_kernel, x_count), out_shape=(jax.S...  77.8 us
    pallas_call x1, Pallas kernels, hand_in(): pl.pallas_call(hand_in_kernel, out_shape=tuple((jax.ShapeDtypeStruct(x.sh...  1.7 us

profile of v5, /device:TPU:1, one launch (start us, length us, event | category | flops | bytes accessed | tf_op | source)
XLA Modules:
  0.0 80.2 jit_solution(8652405305807922083)
XLA Ops:
  0.6 77.8 %shard_map.84 = (bf16[128,512]{1,0:T(8,128)(2,1)}, bf16[128,512]{1,0:T(8,128)(2,1)}, bf16[128,128]{1,0:T(8,128)(2,1)}, bf16[128,128]{1,0:T(8,128)(2,1)}) custom-call(s32[8192]{0:T(1024)} %pos_ref.1, bf16[16,4096]{1,0:T(8,128)(2,1)} %q_ref.1, bf16[16,1024]{1,0:T(8,128)(2,1)} %k_ref.1, bf16[16,1024]{1,0:T(8,128)(2,1)} %v_ref.1, bf16[128,512]{1,0:T(8,128)(2,1)} %do_ref.1), custom_call_target="tpu_custom_call" | custom-call | tf_op jit(solution)/shard_map/pallas_call | solution.py:685
  78.5 1.7 %shard_map.85 = (bf16[128,512]{1,0:T(8,128)(2,1)}, bf16[128,512]{1,0:T(8,128)(2,1)}, bf16[128,128]{1,0:T(8,128)(2,1)}, bf16[128,128]{1,0:T(8,128)(2,1)}) custom-call(bf16[128,512]{1,0:T(8,128)(2,1)} %get-tuple-element.8.refs_0_, bf16[128,512]{1,0:T(8,128)(2,1)} %get-tuple-element.9.refs_1_, bf16[128,128]{1,0:T(8,128)(2,1)} %get-tuple-element.10.refs_2_, ...), custom_call_target="tpu_custom_call" | custom-call | tf_op jit(solution)/shard_map/pallas_call | solution.py:707

commit v6 on v5

--- a/solution.py
+++ b/solution.py
@@ -205,11 +205,11 @@
         for copy in copies:
             copy.wait_recv()
 
-    def move_a(way, step, group):
-        part = kv.at[0, group]
-        if step == far - 1:
-            part = kv.at[0, group, pl.ds(way * (size // 2), size // 2), :]
-        copy = push(part, part, ga[2].at[way, step], ga[3].at[way, step], towards(way))
+    def move_a(way, step, k, group):
+        if step == far - 1 and k != way:
+            return None
+        part = kv.at[0, group, pl.ds(k * (size // 2), size // 2), :]
+        copy = push(part, part, ga[2].at[way, step, k], ga[3].at[way, step, k], towards(way))
         sent.append(copy)
         return copy
 
@@ -231,13 +231,33 @@
         sent.append(copy)
         crosses[half, i] = copy
 
+    def one(src, dst, send, recv, device):
+        copy = push(src, dst, send, recv, device)
+        sent.append(copy)
+        return copy
+
+    pair_start = lax.div(at.x, 2) * (2 * rows)
+    mine_pair = pl.ds(pl.multiple_of(pair_start, 2 * rows), 2 * rows)
+    facing_pair = pl.ds(pl.multiple_of(2 * rows - pair_start, 2 * rows), 2 * rows)
+    beside_me = at.device(x=at.x + 1 - 2 * lax.rem(at.x, 2))
+    facing_me = at.device(x=at.xs - 1 - at.x)
+
     def spread(i, group):
         part = kv.at[1, group, mine, :]
-        return i, group, beside(part, part, gb[0].at[i], gb[1].at[i])
+        return i, group, one(part, part, gb[0].at[i, 0], gb[1].at[i, 0], beside_me)
+
+    def widen(spreads):
+        wider = []
+        for i, group, copy in spreads:
+            copy.wait_recv()
+            part = kv.at[1, group, mine_pair, :]
+            copy = one(part, part, gb[0].at[i, 1], gb[1].at[i, 1], facing_me)
+            wider.append((i, group, copy))
+        return wider
 
     def finish(spreads):
-        for i, group, copies in spreads:
-            arrive(copies)
+        for i, group, copy in spreads:
+            copy.wait_recv()
             cross(1, i, group)
 
     def fold(x, op):
@@ -360,8 +380,9 @@
     b_moves = [move_b(way, 0, own) for way in range(2)]
     spreads = [spread(0, own)]
     arrive(a_first)
-    a_moves = [move_a(way, 0, own) for way in range(2)]
+    a_moves = [[move_a(way, 0, k, own) for way in range(2)] for k in range(2)]
     cross(0, 0, own)
+    spreads = widen(spreads)
     arrive(q_moves)
     for s in range(2):
         for h in range(RATIO):
@@ -398,14 +419,18 @@
         else:
             b_moves = [move_b(way, step + 1, groups[way]) for way in range(2)]
             spreads = [spread(2 * step + 1 + way, groups[way]) for way in range(2)]
+        for k in range(2):
+            for way in range(2):
+                if a_moves[k][way] is not None:
+                    a_moves[k][way].wait_recv()
+                if not last:
+                    a_moves[k][way] = move_a(way, step + 1, k, groups[way])
         if last:
-            arrive(a_moves)
             cross(0, 2 * far - 1, groups[0])
         else:
             for way in range(2):
-                a_moves[way].wait_recv()
-                a_moves[way] = move_a(way, step + 1, groups[way])
                 cross(0, 2 * step + 1 + way, groups[way])
+        spreads = widen(spreads)
         if step == 0:
             crossed([0])
             forward(1, 1, lambda j: at.group(at.z, 1 - at.core))
@@ -514,11 +539,32 @@
         sent.extend(copies)
         return copies
 
-    def spread_b(i):
-        both_cores = pair(1, i)
-        keep[i] = both_cores
-        xb_out[i] = both_cores.astype(BF16)
-        return across(xb_out.at[i], xb_in.at[i], sb[0].at[i], sb[1].at[i])
+    def first_b(i):
+        keep[i] = pair(1, i)
+        xb_out[i, : 2 * rows, :] = keep[i, facing_pair, :].astype(BF16)
+        b_copies[i] = one(
+            xb_out.at[i, pl.ds(0, 2 * rows), :],
+            xb_in.at[i, pl.ds(0, 2 * rows), :],
+            sb[0].at[i, 0],
+            sb[1].at[i, 0],
+            facing_me,
+        )
+
+    def second_b(i):
+        b_copies[i].wait_recv()
+        summed = keep[i, mine_pair, :] + xb_in[i, : 2 * rows, :].astype(F32)
+        keep[i, mine_pair, :] = summed
+        xb_out[i, 2 * rows :, :] = summed.astype(BF16)
+        theirs = 2 * rows + (1 - lax.rem(at.x, 2)) * rows
+        b_copies[i] = one(
+            xb_out.at[i, pl.ds(pl.multiple_of(theirs, rows), rows), :],
+            xb_in.at[i, pl.ds(2 * rows, rows), :],
+            sb[0].at[i, 1],
+            sb[1].at[i, 1],
+            beside_me,
+        )
+
+    b_copies = {}
 
     def collect(copies, kept, arrived):
         summed = kept[mine, :]
@@ -528,45 +574,45 @@
         return summed
 
     def collect_b(i):
-        return collect(b_spreads[i], keep.at[i], xb_in.at[i])
+        b_copies[i].wait_recv()
+        return keep[i, mine, :] + xb_in[i, 2 * rows : 3 * rows, :].astype(F32)
 
     def half_of(way, length):
         return slice(way * (length // 2), (way + 1) * (length // 2))
 
-    def along(out, into, sems, way, step):
+    def along(out, into, sems, way, step, k):
         length = out.shape[2]
-        place = pl.ds(way * (length // 2), length // 2) if step == 0 else pl.ds(0, length)
-        copy = push(
+        place = pl.ds(k * (length // 2), length // 2)
+        return one(
             out.at[way, step, place, :],
             into.at[way, step, place, :],
-            sems[2].at[way, step],
-            sems[3].at[way, step],
+            sems[2].at[way, step, k],
+            sems[3].at[way, step, k],
             towards(way),
         )
-        sent.append(copy)
-        return copy
 
     def begin(summed, out, into, sems):
-        moves = []
+        moves = [[None, None], [None, None]]
         for way in range(2):
             place = half_of(way, out.shape[2])
             out[way, 0, place, :] = summed[place].astype(BF16)
-            moves.append(along(out, into, sems, way, 0))
+            moves[way][way] = along(out, into, sems, way, 0, way)
         return moves
 
     def go_on(moves, way, step, summed, out, into, sems):
-        moves[way].wait_recv()
-        if step == 1:
-            near, rest = half_of(way, out.shape[2]), half_of(1 - way, out.shape[2])
-            out[way, 1, near, :] = (summed[near] + into[way, 0, near, :].astype(F32)).astype(BF16)
-            out[way, 1, rest, :] = summed[rest].astype(BF16)
-        else:
-            out[way, step] = (summed + into[way, step - 1].astype(F32)).astype(BF16)
-        moves[way] = along(out, into, sems, way, step)
+        for k in (1 - way, way):
+            place = half_of(k, out.shape[2])
+            value = summed[place]
+            if moves[way][k] is not None:
+                moves[way][k].wait_recv()
+                value = value + into[way, step - 1, place, :].astype(F32)
+            out[way, step, place, :] = value.astype(BF16)
+            moves[way][k] = along(out, into, sems, way, step, k)
 
     def end(moves, summed, into):
         for way in range(2):
-            moves[way].wait_recv()
+            for k in range(2):
+                moves[way][k].wait_recv()
             summed = summed + into[way, far - 1].astype(F32)
         return summed
 
@@ -586,34 +632,40 @@
     backward(at.group(at.z_off(far), 1 - at.core), 1 + far, 0, 0)
     give(0)
     backward(at.group(at.z_off(far), at.core), 1 + far, 1, 0)
-    b_spreads = {0: spread_b(0)}
+    first_b(0)
     a_moves = begin(pair(0, 0), *a_refs)
     b_moves = None
     for step in range(1, far):
+        before = [0] if step == 1 else [2 * step - 3, 2 * step - 2]
+        here = [2 * step - 1, 2 * step]
         back(0, step)
-        give(2 * step - 1)
-        give(2 * step)
+        for i in here:
+            give(i)
+        for i in before:
+            second_b(i)
         back(1, step)
+        for i in here:
+            first_b(i)
         for way in range(2):
-            b_spreads[2 * step - 1 + way] = spread_b(2 * step - 1 + way)
-        for way in range(2):
-            go_on(a_moves, way, step, pair(0, 2 * step - 1 + way), *a_refs)
+            go_on(a_moves, way, step, pair(0, here[way]), *a_refs)
         if step == 1:
             b_moves = begin(collect_b(0), *b_refs)
         else:
             for way in range(2):
-                go_on(b_moves, way, step - 1, collect_b(2 * step - 3 + way), *b_refs)
+                go_on(b_moves, way, step - 1, collect_b(before[way]), *b_refs)
     backward(at.group(at.z, 1 - at.core), 1, 0, at.zs - 1)
     give(at.zs - 1)
+    for i in here:
+        second_b(i)
+    backward_own(at.zs - 1)
+    first_b(at.zs - 1)
     for way in range(2):
-        go_on(b_moves, way, far - 1, collect_b(2 * far - 3 + way), *b_refs)
-    backward_own(at.zs - 1)
-    b_spreads[at.zs - 1] = spread_b(at.zs - 1)
+        go_on(b_moves, way, far - 1, collect_b(here[way]), *b_refs)
     mine_a = end(a_moves, pair(0, at.zs - 1), za_in)
-    other_a = keep.at[0]
-    other_a[...] = mine_a
+    keep[0] = mine_a
     xa_out[...] = mine_a.astype(BF16)
     last_a = across(xa_out, xa_in, sa[0], sa[1])
+    second_b(at.zs - 1)
     for s in range(2):
         grad = (acc_dq[part(s), :] * (total[s, 0:1, :] * SCALE)).T.astype(BF16)
         for h in range(RATIO):
@@ -641,8 +693,9 @@
     dma = pltpu.SemaphoreType.DMA
     vmem = pl.BlockSpec(memory_space=pltpu.VMEM)
     sems = [(3, heads - 1), (3, heads - 1)]
-    for x_dims in ((x_count - 1,), (zs, x_count - 1)) * 2:
-        sems += [x_dims, x_dims, (2, far), (2, far), (zs,), (zs,)]
+    for x_dims, z_dims in (((x_count - 1,), (2, far, 2)), ((zs, 2), (2, far))) * 2:
+        sems += [x_dims, x_dims, z_dims, z_dims, (zs,), (zs,)]
+    sems[-4:-2] = [(2, far, 2)] * 2
     buffers = [
         ((rows, width), BF16),
         ((rows, kv_width), BF16),
@@ -678,7 +731,7 @@
         ((2, far, run, kv_width), BF16),
         ((x_count - 1, run, kv_width), BF16),
         ((size, kv_width), BF16),
-        ((zs, x_count - 1, run, kv_width), BF16),
+        ((zs, 3 * run, kv_width), BF16),
         ((zs, size, kv_width), BF16),
         ((zs, size, kv_width), F32),
     ]

time: 80.4 us -> 95.6 us (1.19)
  the two profiles are of different devices: /device:TPU:1 before, /device:TPU:2 now
where the time goes in v6:
time: 95.6 us; the launch traced here: 95.4 us
  Pallas kernels  94.8 us (99%)
    pallas_call x1, Pallas kernels, layer(): pl.pallas_call(functools.partial(layer_kernel, x_count), out_shape=(jax.S...  93.1 us

profile of v6, /device:TPU:2, one launch (start us, length us, event | category | flops | bytes accessed | tf_op | source)
XLA Modules:
  0.0 95.4 jit_solution(7040133513635882152)
XLA Ops:
  0.6 93.1 %shard_map.84 = (bf16[128,512]{1,0:T(8,128)(2,1)}, bf16[128,512]{1,0:T(8,128)(2,1)}, bf16[128,128]{1,0:T(8,128)(2,1)}, bf16[128,128]{1,0:T(8,128)(2,1)}) custom-call(s32[8192]{0:T(1024)} %pos_ref.1, bf16[16,4096]{1,0:T(8,128)(2,1)} %q_ref.1, bf16[16,1024]{1,0:T(8,128)(2,1)} %k_ref.1, bf16[16,1024]{1,0:T(8,128)(2,1)} %v_ref.1, bf16[128,512]{1,0:T(8,128)(2,1)} %do_ref.1), custom_call_target="tpu_custom_call" | custom-call | tf_op jit(solution)/shard_map/pallas_call | solution.py:738
  93.7 1.7 %shard_map.85 = (bf16[128,512]{1,0:T(8,128)(2,1)}, bf16[128,512]{1,0:T(8,128)(2,1)}, bf16[128,128]{1,0:T(8,128)(2,1)}, bf16[128,128]{1,0:T(8,128)(2,1)}) custom-call(bf16[128,512]{1,0:T(8,128)(2,1)} %get-tuple-element.8.refs_0_, bf16[128,512]{1,0:T(8,128)(2,1)} %get-tuple-element.9.refs_1_, bf16[128,128]{1,0:T(8,128)(2,1)} %get-tuple-element.10.refs_2_, ...), custom_call_target="tpu_custom_call" | custom-call | tf_op jit(solution)/shard_map/pallas_call | solution.py:760

commit v7 on v5

--- a/solution.py
+++ b/solution.py
@@ -391,20 +391,19 @@
     for step in range(far):
         groups = [at.group(at.z_off((2 * way - 1) * (step + 1)), at.core) for way in range(2)]
         last = step == far - 1
-        spreads = []
-        arrive(b_moves)
         if last:
-            spreads.append(spread(2 * far - 1, groups[0]))
-        else:
-            b_moves = [move_b(way, step + 1, groups[way]) for way in range(2)]
-            spreads = [spread(2 * step + 1 + way, groups[way]) for way in range(2)]
-        if last:
+            arrive(b_moves)
+            spreads = [spread(2 * far - 1, groups[0])]
             arrive(a_moves)
             cross(0, 2 * far - 1, groups[0])
         else:
             for way in range(2):
                 a_moves[way].wait_recv()
                 a_moves[way] = move_a(way, step + 1, groups[way])
+            arrive(b_moves)
+            b_moves = [move_b(way, step + 1, groups[way]) for way in range(2)]
+            spreads = [spread(2 * step + 1 + way, groups[way]) for way in range(2)]
+            for way in range(2):
                 cross(0, 2 * step + 1 + way, groups[way])
         if step == 0:
             crossed([0])
@@ -413,25 +412,37 @@
             crossed([2 * step - 1, 2 * step])
             forward(1 + step, 4, both(step))
         finish(spreads)
+    farthest = [at.group(at.z_off(far), core) for core in (at.core, 1 - at.core)]
+    score(0, farthest[0])
     crossed([2 * far - 1])
-    forward(1 + far, 2, lambda j: at.group(at.z_off(far), lax.rem(at.core + j, 2)))
+    score(1, farthest[1])
+    renew(1 + far)
+    for j in range(2):
+        weigh(j, farthest[j])
+
+    def output(s):
+        return (acc_out[part(s), :] * total[s, 0:1, :]).astype(BF16).astype(F32)
+
+    def emit_output():
+        for s in range(2):
+            out = output(s).T.astype(BF16)
+            for h in range(RATIO):
+                out_ref[run(s), h * DH : (h + 1) * DH] = out[run(h)]
+
+    def scale(batch):
+        for s in range(2):
+            factor = jnp.exp2((marks[batch, s] - peak[s]) * (SCALE * LOG2E))
+            marks[batch, s] = factor
+            by_row = jnp.broadcast_to(factor[0:1] * total[s, 0:1, :], (DH, ROWS)).T
+            dod[batch, :, part(s)] = (dos[:, part(s)].astype(F32) * by_row).astype(BF16)
+            qd[batch, :, part(s)] = (qs[:, part(s)].astype(F32) * (by_row * SCALE)).astype(BF16)
 
     for s in range(2):
         inv = 1.0 / jnp.sum(total[s], axis=0, keepdims=True)
-        out = (acc_out[part(s), :] * inv).astype(BF16).astype(F32)
+        total[s] = jnp.broadcast_to(inv, (8, ROWS))
         d_rows = dos[:, part(s)].astype(F32)
-        q_part = qs[:, part(s)].astype(F32) * SCALE
-        delta[s] = jnp.broadcast_to(jnp.sum(out * d_rows.T, axis=0, keepdims=True), (8, ROWS))
-        total[s] = jnp.broadcast_to(inv, (8, ROWS))
-        for batch in range(far + 2):
-            factor = jnp.exp2((marks[batch, s] - peak[s]) * (SCALE * LOG2E))
-            marks[batch, s] = factor
-            by_row = jnp.broadcast_to(factor[0:1] * inv, (DH, ROWS)).T
-            dod[batch, :, part(s)] = (d_rows * by_row).astype(BF16)
-            qd[batch, :, part(s)] = (q_part * by_row).astype(BF16)
-        out = out.T.astype(BF16)
-        for h in range(RATIO):
-            out_ref[run(s), h * DH : (h + 1) * DH] = out[run(h)]
+        delta[s] = jnp.broadcast_to(jnp.sum(output(s) * d_rows.T, axis=0, keepdims=True), (8, ROWS))
+    scale(1 + far)
 
     def backward(group, batch, who, i):
         full, mix = e_full[group], e_mix[group]
@@ -588,6 +599,9 @@
     backward(at.group(at.z_off(far), at.core), 1 + far, 1, 0)
     b_spreads = {0: spread_b(0)}
     a_moves = begin(pair(0, 0), *a_refs)
+    for batch in range(1 + far):
+        scale(batch)
+    emit_output()
     b_moves = None
     for step in range(1, far):
         back(0, step)

time: 80.4 us -> 82.1 us (1.021)
  Pallas kernels: 79.5 us -> 81.2 us
    pallas_call x1, Pallas kernels: 77.8 us -> 79.5 us  [layer(): pl.pallas_call(functools.partial(layer_kernel, x_count), out_shape=(jax.S...]
where the time goes in v7:
time: 82.1 us; the launch traced here: 81.9 us
  Pallas kernels  81.2 us (99%)
    pallas_call x1, Pallas kernels, layer(): pl.pallas_call(functools.partial(layer_kernel, x_count), out_shape=(jax.S...  79.5 us
    pallas_call x1, Pallas kernels, hand_in(): pl.pallas_call(hand_in_kernel, out_shape=tuple((jax.ShapeDtypeStruct(x.sh...  1.7 us

profile of v7, /device:TPU:1, one launch (start us, length us, event | category | flops | bytes accessed | tf_op | source)
XLA Modules:
  0.0 81.9 jit_solution(2010389535855387979)
XLA Ops:
  0.6 79.5 %shard_map.84 = (bf16[128,512]{1,0:T(8,128)(2,1)}, bf16[128,512]{1,0:T(8,128)(2,1)}, bf16[128,128]{1,0:T(8,128)(2,1)}, bf16[128,128]{1,0:T(8,128)(2,1)}) custom-call(s32[8192]{0:T(1024)} %pos_ref.1, bf16[16,4096]{1,0:T(8,128)(2,1)} %q_ref.1, bf16[16,1024]{1,0:T(8,128)(2,1)} %k_ref.1, bf16[16,1024]{1,0:T(8,128)(2,1)} %v_ref.1, bf16[128,512]{1,0:T(8,128)(2,1)} %do_ref.1), custom_call_target="tpu_custom_call" | custom-call | tf_op jit(solution)/shard_map/pallas_call | solution.py:699
  80.2 1.7 %shard_map.85 = (bf16[128,512]{1,0:T(8,128)(2,1)}, bf16[128,512]{1,0:T(8,128)(2,1)}, bf16[128,128]{1,0:T(8,128)(2,1)}, bf16[128,128]{1,0:T(8,128)(2,1)}) custom-call(bf16[128,512]{1,0:T(8,128)(2,1)} %get-tuple-element.8.refs_0_, bf16[128,512]{1,0:T(8,128)(2,1)} %get-tuple-element.9.refs_1_, bf16[128,128]{1,0:T(8,128)(2,1)} %get-tuple-element.10.refs_2_, ...), custom_call_target="tpu_custom_call" | custom-call | tf_op jit(solution)/shard_map/pallas_call | solution.py:721
